TPU v7x, 32 devices: a whole 2x2x4 slice. The times are simulated.
32 devices in a mesh: tmpl: 8 (over z, core), chan: 4 (over y, x).
Axes of the slice: x: 2, y: 2, z: 4, core: 2. Of those that a mesh axis runs over, the one named last changes fastest.
Arguments:
- data: bfloat16 [8, 96, 2304], P('tmpl', 'chan')
- templates: bfloat16 [2048, 96, 200], P('tmpl', 'chan')
- counts: int32 [8], P('tmpl'), may hold values from 32 to 256, as said below
- owners: int32 [3], replicated, may hold values from 0 to 7
Outputs:
- traces: float32 [2048, 3, 2048], P('tmpl', None, 'chan')
Inputs may be any that keep to these rules, and one draw needn't show every extreme that they name: `counts`: every count is a multiple of 32; some index of tmpl holds exactly 256 live slots.
All inputs are finite; a program needn't handle non-finite values.
Results may differ from a plain program's by a relative error of at most 0.0041.
Values may be sent and summed in bfloat16 or wider, within the bound.
No kernel may reach another device: no remote copies, remote signals or barrier semaphores. Data moves between devices by JAX's collectives and lax.ppermute only.
A program may use at most 128 MiB of HBM per device.

v0:
```python
import functools
import math

import jax
import jax.numpy as jnp
from jax import lax
from jax.experimental import pallas as pl
from jax.experimental.pallas import tpu as pltpu
from jax.sharding import PartitionSpec as P

W = 200
NB = 3
LO = 2048
TB = 32
EPS = 1e-06
VMEM_LIMIT = 48 * 2**20


def inverse_norm(mean_square):
    return 1.0 / (jnp.sqrt(mean_square + EPS) * math.sqrt(W))


def template_kernel(tpl_ref, out_ref, scaled_ref):
    chans, _, slots = tpl_ref.shape
    for c in range(0, chans, 2):
        pair = []
        for k in (c, c + 1):
            values = tpl_ref[k].astype(jnp.float32)
            mean_square = jnp.sum(values * values, axis=0, keepdims=True) * (1.0 / W)
            pair.append(values * inverse_norm(mean_square))
        scaled_ref[c * W : (c + 2) * W, :] = jnp.concatenate(pair, 0).astype(jnp.bfloat16)
    depth = chans * W
    for at in range(0, depth, slots):
        size = min(slots, depth - at)
        out_ref[:, at : at + size] = scaled_ref[at : at + size, :].T


def normalize_templates(templates):
    slots, chans, _ = templates.shape
    return pl.pallas_call(
        template_kernel,
        out_shape=jax.ShapeDtypeStruct((slots, chans * W), jnp.bfloat16),
        scratch_shapes=[pltpu.VMEM((chans * W, slots), jnp.bfloat16)],
        compiler_params=pltpu.CompilerParams(vmem_limit_bytes=VMEM_LIMIT),
        cost_estimate=pl.CostEstimate(
            flops=4 * slots * chans * W, bytes_accessed=4 * slots * chans * W, transcendentals=0
        ),
        name="normalize_templates",
    )(jnp.transpose(templates, (1, 2, 0)))


def shift_left(x, amount):
    return pltpu.roll(x, x.shape[1] - amount, 1) if amount else x


def block_kernel(code_ref, even_ref, odd_ref, seg_ref, scale_ref):
    chans = even_ref.shape[1]
    lags = scale_ref.shape[2]
    for number in range(NB):
        code = code_ref[number]
        slot = lax.div(code, 2)
        segment = jnp.where(
            lax.rem(code, 2) == 1,
            odd_ref[slot].astype(jnp.float32),
            even_ref[slot].astype(jnp.float32),
        )
        seg_ref[number, :chans, :] = segment.astype(jnp.bfloat16)
        sums = {1: segment * segment}
        for p in range(7):
            sums[2 << p] = sums[1 << p] + shift_left(sums[1 << p], 1 << p)
        total = sums[128] + shift_left(sums[64], 128) + shift_left(sums[8], 192)
        scale_ref[number, :chans, :] = inverse_norm(total[:, :lags] * (1.0 / W))


def choose_blocks(codes, even, odd):
    _, chans, length = even.shape
    held = -(-chans // 8) * 8
    return pl.pallas_call(
        block_kernel,
        out_shape=(
            jax.ShapeDtypeStruct((NB, held, length), jnp.bfloat16),
            jax.ShapeDtypeStruct((NB, held, LO), jnp.float32),
        ),
        in_specs=[
            pl.BlockSpec(memory_space=pltpu.SMEM),
            pl.BlockSpec(memory_space=pltpu.VMEM),
            pl.BlockSpec(memory_space=pltpu.VMEM),
        ],
        compiler_params=pltpu.CompilerParams(vmem_limit_bytes=VMEM_LIMIT),
        cost_estimate=pl.CostEstimate(flops=10**10, bytes_accessed=10**8, transcendentals=0),
        name="choose_blocks",
    )(codes, even, odd)


def build_windows(at, held, chans, base_ref, scale_ref, win_ref):
    lags = win_ref.shape[1]
    tiles = base_ref.shape[0]
    scale = scale_ref[at * held : (at + 1) * held, :]
    for c in range(0, chans, 2):
        rows = []
        for k in (c, c + 1):
            line = (at * held + k) * 8
            base = jnp.concatenate([base_ref[j, line : line + 8, :] for j in range(tiles)], 1)
            row_scale = jnp.broadcast_to(scale[k : k + 1, :], (8, lags))
            wide = [shift_left(base, 8 * g)[:, : lags + 128] for g in range(16)]
            rows += [wide[g][:, :lags] * row_scale for g in range(16)]
            rows += [wide[g][:, 128:] * row_scale for g in range((W - 128) // 8)]
        win_ref[c * W : (c + 2) * W, :] = jnp.concatenate(rows, 0).astype(jnp.bfloat16)


def partial_kernel(chunks, n_add, write, place_ref, tpl_ref, seg_ref, scale_ref, *refs):
    adds, outs = refs[1 : 1 + n_add], refs[1 + n_add : -4]
    seg_now, scale_now, base_now, win_ref = refs[-4:]
    depth, lags = win_ref.shape
    held = seg_ref.shape[1]
    span = seg_now.shape[1]
    for index, number in enumerate(chunks):
        start = pl.multiple_of(place_ref[index] * lags, 128)
        lines = slice(index * held, (index + 1) * held)
        seg_now[lines, :] = seg_ref[number, :, pl.ds(start, span)].astype(jnp.float32)
        scale_now[lines, :] = scale_ref[number, :, pl.ds(start, lags)]
    segment = seg_now[...]
    for s in range(8):
        moved = shift_left(segment, s)
        for j in range(span // 128):
            base_now[j, pl.ds(s, segment.shape[0], stride=8), :] = moved[:, 128 * j : 128 * (j + 1)]
    for index in range(len(chunks)):
        build_windows(index, held, depth // W, base_now, scale_now, win_ref)
        product = jnp.dot(tpl_ref[...], win_ref[...], preferred_element_type=jnp.float32)
        write(index, product, adds, outs)


def partial_sums(chunks, write, outs, place, normed, segments, scales, adds=(), order=None):
    lags = outs[0].shape[-1]
    depth = normed.shape[1]
    held = segments.shape[1]
    whole = pl.BlockSpec(memory_space=pltpu.VMEM)
    order = place if order is None else order
    return pl.pallas_call(
        functools.partial(partial_kernel, chunks, len(adds), write),
        out_shape=outs,
        in_specs=[
            pl.BlockSpec(memory_space=pltpu.SMEM),
            whole,
            whole,
            whole,
            pl.BlockSpec(memory_space=pl.ANY),
        ]
        + [whole] * len(adds),
        scratch_shapes=[
            pltpu.VMEM((len(chunks) * held, lags + 256), jnp.float32),
            pltpu.VMEM((len(chunks) * held, lags), jnp.float32),
            pltpu.VMEM(((lags + 256) // 128, len(chunks) * held * 8, 128), jnp.float32),
            pltpu.VMEM((depth, lags), jnp.bfloat16),
        ],
        compiler_params=pltpu.CompilerParams(vmem_limit_bytes=VMEM_LIMIT),
        cost_estimate=pl.CostEstimate(flops=10**12, bytes_accessed=10**10, transcendentals=0),
        name="partial_sums",
    )(place, normed, segments, scales, order, *adds)


def write_plain(index, product, adds, outs):
    outs[0][index] = product.astype(outs[0].dtype)


def write_halves(index, product, adds, outs):
    half = outs[0].shape[1]
    outs[0][index] = product[:half].astype(jnp.bfloat16)
    outs[1][index] = product[half:].astype(jnp.bfloat16)


def write_added(at, index, product, adds, outs):
    half = product.shape[0] // 2
    here = adds[index][at].astype(jnp.float32)
    if index == 0:
        outs[0][:half] = product[:half].astype(jnp.bfloat16)
        outs[0][half:] = (product[half:] + here).astype(jnp.bfloat16)
    else:
        outs[1][:half] = (product[:half] + here).astype(jnp.bfloat16)
        outs[1][half:] = product[half:].astype(jnp.bfloat16)


def exchange(value, step, n_chan):
    return lax.ppermute(value, "chan", [(i, i ^ step) for i in range(n_chan)])


def two_steps(normed, segments, scales, lags):
    slots = normed.shape[0]
    me = lax.axis_index("chan")
    args = (normed, segments, scales)

    def message(count, rows):
        return jax.ShapeDtypeStruct((count, rows, lags), jnp.bfloat16)

    via_x, via_y = [], []
    order = None
    for chunks in ((0,), (1, 2)):
        out = (message(len(chunks), slots // 2),) * 2
        place = jnp.stack([me ^ 3] * len(chunks))
        upper, lower = partial_sums(chunks, write_halves, out, place, *args, order=order)
        order = lower
        via_x.append(exchange(upper, 1, 4))
        via_y.append(exchange(lower, 2, 4))
    arrived = []
    place = jnp.stack([me ^ 1, me ^ 2])
    for number in range(NB):
        part, at = (0, 0) if number == 0 else (1, number - 1)
        out = (jax.ShapeDtypeStruct((slots, lags), jnp.bfloat16),) * 2
        to_x, to_y = partial_sums(
            (number, number),
            functools.partial(write_added, at),
            out,
            place,
            *args,
            adds=(via_y[part], via_x[part]),
            order=order,
        )
        order = to_y
        arrived.append((exchange(to_x, 1, 4), exchange(to_y, 2, 4)))
    out = (jax.ShapeDtypeStruct((NB, slots, lags), jnp.float32),)
    (total,) = partial_sums(
        tuple(range(NB)), write_plain, out, jnp.stack([me] * NB), *args, order=order
    )
    return total, [jnp.stack([pair[side] for pair in arrived]) for side in range(2)]


def one_step(normed, segments, scales, lags, n_chan):
    slots = normed.shape[0]
    me = lax.axis_index("chan")
    every = tuple(range(NB))
    arrived = []
    order = None
    for step in range(n_chan - 1, -1, -1):
        dtype = jnp.bfloat16 if step else jnp.float32
        out = (jax.ShapeDtypeStruct((NB, slots, lags), dtype),)
        place = jnp.stack([me ^ step] * NB)
        (order,) = partial_sums(
            every, write_plain, out, place, normed, segments, scales, order=order
        )
        if step:
            arrived.append(exchange(order, step, n_chan))
    return order, arrived


def body(n_tmpl, n_chan, data, templates, counts, owners):
    lags = LO // n_chan
    parts = [data]
    for step in range(2, n_tmpl, 2):
        parts.append(lax.ppermute(data, "tmpl", [(i, i ^ step) for i in range(n_tmpl)]))
    normed = normalize_templates(templates)
    even, normed = lax.optimization_barrier((jnp.concatenate(parts, 0), normed))
    odd = lax.ppermute(even, "tmpl", [(i, i ^ 1) for i in range(n_tmpl)])
    codes = owners ^ lax.axis_index("tmpl")
    segments, scales = choose_blocks(codes, even, odd)
    if n_chan == 4:
        total, arrived = two_steps(normed, segments, scales, lags)
    else:
        total, arrived = one_step(normed, segments, scales, lags, n_chan)
    for part in arrived:
        total = total + part.astype(jnp.float32)
    live = lax.broadcasted_iota(jnp.int32, total.shape, 1) < counts[0]
    return jnp.transpose(jnp.where(live, total, 0.0), (1, 0, 2))


def solution(mesh):
    placed = (P("tmpl", "chan", None), P("tmpl", "chan", None), P("tmpl"), P())
    return jax.shard_map(
        functools.partial(body, mesh.shape["tmpl"], mesh.shape["chan"]),
        mesh=mesh,
        in_specs=placed,
        out_specs=P("tmpl", None, "chan"),
        check_vma=False,
    )
```

profile of v0, /device:TPU:0, one launch (start us, length us, event | category | flops | bytes accessed | tf_op | source)
XLA Modules:
  0.0 66.1 jit_solution(12944580369081669706)
XLA Ops:
  0.0 3.0 %collective-permute-start = (bf16[1,24,2304]{2,1,0:T(8,128)(2,1)}, bf16[1,24,2304]{2,1,0:T(8,128)(2,1)S(1)}, u32[]{:S(2)}, u32[]{:S(2)}) collective-permute-start(bf16[1,24,2304]{2,1,0:T(8,128)(2,1)} %param.4), channel_id=1, source_target_pairs={{0,8},{4,12},{8,0},{12,4},{16,24},{20,28},{24,16},{28,20},{1,9},{5... | collective-permute-start | bytes 331784 | tf_op jit(solution)/shard_map/ppermute | solution.py:249
  3.0 2.6 %collective-permute-start.1 = (bf16[1,24,2304]{2,1,0:T(8,128)(2,1)}, bf16[1,24,2304]{2,1,0:T(8,128)(2,1)S(1)}, u32[]{:S(2)}, u32[]{:S(2)}) collective-permute-start(bf16[1,24,2304]{2,1,0:T(8,128)(2,1)} %param.4), channel_id=1, source_target_pairs={{0,16},{4,20},{8,24},{12,28},{16,0},{20,4},{24,8},{28,12},{1,17},{... | collective-permute-start | bytes 331784 | tf_op jit(solution)/shard_map/ppermute | solution.py:249
  5.6 1.7 %copy-done = bf16[256,24,200]{0,2,1:T(8,128)(2,1)S(1)} copy-done((bf16[256,24,200]{0,2,1:T(8,128)(2,1)S(1)}, bf16[256,24,200]{0,2,1:T(8,128)(2,1)}, u32[]{:S(2)}) %copy-start) | copy-done | bytes 2457624
  7.3 0.8 %normalize_templates.1.tpl_ref = bf16[256,4800]{1,0:T(8,128)(2,1)S(1)} custom-call(bf16[24,200,256]{2,1,0:T(8,128)(2,1)S(1)} %bitcast.14), custom_call_target="tpu_custom_call" | custom-call | flops 4915200 | bytes 4915200 | tf_op jit(solution)/shard_map/normalize_templates/pallas_call | solution.py:40
  8.8 0.1 pad_add_fusion.1.place_ref
  8.9 5.7 %collective-permute-done.1 = bf16[1,24,2304]{2,1,0:T(8,128)(2,1)S(1)} collective-permute-done((bf16[1,24,2304]{2,1,0:T(8,128)(2,1)}, bf16[1,24,2304]{2,1,0:T(8,128)(2,1)S(1)}, u32[]{:S(2)}, u32[]{:S(2)}) %collective-permute-start.1) | collective-permute-done | bytes 110624 | tf_op jit(solution)/shard_map/ppermute | solution.py:249
  14.6 0.0 collective-permute-done.2
  14.6 0.1 pad_maximum_fusion.even_ref
  14.7 0.1 collective-permute-start.3
  14.7 0.6 iota_compare_fusion
  15.3 0.1 pad_add_fusion.place_ref
  15.4 1.1 %collective-permute-done.3.odd_ref = bf16[4,24,2304]{2,1,0:T(8,128)(2,1)S(1)} collective-permute-done((bf16[4,24,2304]{2,1,0:T(8,128)(2,1)S(1)}, bf16[4,24,2304]{2,1,0:T(8,128)(2,1)S(1)}, u32[]{:S(2)}, u32[]{:S(2)}) %collective-permute-start.3) | collective-permute-done | bytes 442400 | tf_op jit(solution)/shard_map/ppermute | solution.py:252
  16.5 2.3 %choose_blocks.1 = (bf16[3,24,2304]{2,1,0:T(8,128)(2,1)S(1)}, f32[3,24,2048]{2,1,0:T(8,128)S(1)}) custom-call(s32[3]{0:T(128)S(1)} %broadcast_xor_fusion.code_ref, bf16[4,24,2304]{2,1,0:T(8,128)(2,1)S(1)} %pad_maximum_fusion.even_ref, bf16[4,24,2304]{2,1,0:T(8,128)(2,1)S(1)} %collective-permute-done.3.odd_ref), custom_call_target="tpu_custom_call" | custom-call | flops 10000000000 | bytes 100000000 | tf_op jit(solution)/shard_map/choose_blocks/pallas_call | solution.py:78
  18.8 2.6 %partial_sums.6 = (bf16[1,128,512]{2,1,0:T(8,128)(2,1)}, bf16[1,128,512]{2,1,0:T(8,128)(2,1)}) custom-call(s32[1]{0:T(128)} %bitcast.4.place_ref.refs_0_, bf16[256,4800]{1,0:T(8,128)(2,1)S(1)} %normalize_templates.1.tpl_ref, bf16[3,24,2304]{2,1,0:T(8,128)(2,1)S(1)} %get-tuple-element.21.seg_ref, f32[3,24,2048]{2,1,0:T(8,128)S(1)} %get-tuple-element.22.scale_ref, ...), custom_call_target="tpu_custom_call" | custom-call | flops 999999995904 | bytes 10000000000 | tf_op jit(solution)/shard_map/partial_sums/pallas_call | solution.py:139
  21.4 1.6 %collective-permute-start.4 = (bf16[1,128,512]{2,1,0:T(8,128)(2,1)}, bf16[1,128,512]{2,1,0:T(8,128)(2,1)}, u32[]{:S(2)}, u32[]{:S(2)}) collective-permute-start(bf16[1,128,512]{2,1,0:T(8,128)(2,1)} %get-tuple-element.23.refs_0_), channel_id=1, source_target_pairs={{0,2},{1,3},{2,0},{3,1},{4,6},{5,7},{6,4},{7,5},{8,10},{9,11},{10,... | collective-permute-start | bytes 393224 | tf_op jit(solution)/shard_map/ppermute | solution.py:184
  23.0 1.5 %collective-permute-start.5 = (bf16[1,128,512]{2,1,0:T(8,128)(2,1)}, bf16[1,128,512]{2,1,0:T(8,128)(2,1)}, u32[]{:S(2)}, u32[]{:S(2)}) collective-permute-start(bf16[1,128,512]{2,1,0:T(8,128)(2,1)} %get-tuple-element.25), channel_id=1, source_target_pairs={{0,1},{1,0},{2,3},{3,2},{4,5},{5,4},{6,7},{7,6},{8,9},{9,8},{10,11... | collective-permute-start | bytes 393224 | tf_op jit(solution)/shard_map/ppermute | solution.py:184
  24.5 4.8 %partial_sums.7 = (bf16[2,128,512]{2,1,0:T(8,128)(2,1)}, bf16[2,128,512]{2,1,0:T(8,128)(2,1)}) custom-call(s32[2]{0:T(128)S(1)} %pad_add_fusion.1.place_ref, bf16[256,4800]{1,0:T(8,128)(2,1)S(1)} %normalize_templates.1.tpl_ref, bf16[3,24,2304]{2,1,0:T(8,128)(2,1)S(1)} %get-tuple-element.21.seg_ref, f32[3,24,2048]{2,1,0:T(8,128)S(1)} %get-tuple-element.22.scale_ref, ...), custom_call_target="tpu_custom_call" | custom-call | flops 999999995904 | bytes 10000000000 | tf_op jit(solution)/shard_map/partial_sums/pallas_call | solution.py:139
  29.3 0.5 collective-permute-start.6
  29.8 0.5 collective-permute-start.7
  30.3 5.2 %partial_sums.8 = (bf16[256,512]{1,0:T(8,128)(2,1)}, bf16[256,512]{1,0:T(8,128)(2,1)}) custom-call(s32[2]{0:T(128)S(1)} %pad_add_fusion.place_ref, bf16[256,4800]{1,0:T(8,128)(2,1)S(1)} %normalize_templates.1.tpl_ref, bf16[3,24,2304]{2,1,0:T(8,128)(2,1)S(1)} %get-tuple-element.21.seg_ref, f32[3,24,2048]{2,1,0:T(8,128)S(1)} %get-tuple-element.22.scale_ref, ...), custom_call_target="tpu_custom_call" | custom-call | flops 999999995904 | bytes 10000000000 | tf_op jit(solution)/shard_map/partial_sums/pallas_call | solution.py:139
  35.5 1.5 %collective-permute-start.8 = (bf16[256,512]{1,0:T(8,128)(2,1)}, bf16[256,512]{1,0:T(8,128)(2,1)}, u32[]{:S(2)}, u32[]{:S(2)}) collective-permute-start(bf16[256,512]{1,0:T(8,128)(2,1)} %get-tuple-element.30), channel_id=1, source_target_pairs={{0,1},{1,0},{2,3},{3,2},{4,5},{5,4},{6,7},{7,6},{8,9},{9,8},{10,11... | collective-permute-start | bytes 786440 | tf_op jit(solution)/shard_map/ppermute | solution.py:184
  37.0 1.5 %collective-permute-start.11 = (bf16[256,512]{1,0:T(8,128)(2,1)}, bf16[256,512]{1,0:T(8,128)(2,1)}, u32[]{:S(2)}, u32[]{:S(2)}) collective-permute-start(bf16[256,512]{1,0:T(8,128)(2,1)} %get-tuple-element.26.refs_0_), channel_id=1, source_target_pairs={{0,2},{1,3},{2,0},{3,1},{4,6},{5,7},{6,4},{7,5},{8,10},{9,11},{10,... | collective-permute-start | bytes 786440 | tf_op jit(solution)/shard_map/ppermute | solution.py:184
  38.5 5.5 %partial_sums.9 = (bf16[256,512]{1,0:T(8,128)(2,1)}, bf16[256,512]{1,0:T(8,128)(2,1)}) custom-call(s32[2]{0:T(128)S(1)} %pad_add_fusion.place_ref, bf16[256,4800]{1,0:T(8,128)(2,1)S(1)} %normalize_templates.1.tpl_ref, bf16[3,24,2304]{2,1,0:T(8,128)(2,1)S(1)} %get-tuple-element.21.seg_ref, f32[3,24,2048]{2,1,0:T(8,128)S(1)} %get-tuple-element.22.scale_ref, ...), custom_call_target="tpu_custom_call" | custom-call | flops 999999995904 | bytes 10000000000 | tf_op jit(solution)/shard_map/partial_sums/pallas_call | solution.py:139
  44.0 0.7 %collective-permute-start.12 = (bf16[256,512]{1,0:T(8,128)(2,1)}, bf16[256,512]{1,0:T(8,128)(2,1)}, u32[]{:S(2)}, u32[]{:S(2)}) collective-permute-start(bf16[256,512]{1,0:T(8,128)(2,1)} %get-tuple-element.28.refs_0_), channel_id=1, source_target_pairs={{0,2},{1,3},{2,0},{3,1},{4,6},{5,7},{6,4},{7,5},{8,10},{9,11},{10,... | collective-permute-start | bytes 786440 | tf_op jit(solution)/shard_map/ppermute | solution.py:184
  44.7 5.2 %partial_sums.10 = (bf16[256,512]{1,0:T(8,128)(2,1)}, bf16[256,512]{1,0:T(8,128)(2,1)}) custom-call(s32[2]{0:T(128)S(1)} %pad_add_fusion.place_ref, bf16[256,4800]{1,0:T(8,128)(2,1)S(1)} %normalize_templates.1.tpl_ref, bf16[3,24,2304]{2,1,0:T(8,128)(2,1)S(1)} %get-tuple-element.21.seg_ref, f32[3,24,2048]{2,1,0:T(8,128)S(1)} %get-tuple-element.22.scale_ref, ...), custom_call_target="tpu_custom_call" | custom-call | flops 999999995904 | bytes 10000000000 | tf_op jit(solution)/shard_map/partial_sums/pallas_call | solution.py:139
  50.0 1.3 %collective-permute-start.13 = (bf16[256,512]{1,0:T(8,128)(2,1)}, bf16[256,512]{1,0:T(8,128)(2,1)}, u32[]{:S(2)}, u32[]{:S(2)}) collective-permute-start(bf16[256,512]{1,0:T(8,128)(2,1)} %get-tuple-element.29.refs_0_), channel_id=1, source_target_pairs={{0,2},{1,3},{2,0},{3,1},{4,6},{5,7},{6,4},{7,5},{8,10},{9,11},{10,... | collective-permute-start | bytes 786440 | tf_op jit(solution)/shard_map/ppermute | solution.py:184
  51.3 0.5 collective-permute-start.10
  51.8 1.5 %collective-permute-start.9 = (bf16[256,512]{1,0:T(8,128)(2,1)}, bf16[256,512]{1,0:T(8,128)(2,1)}, u32[]{:S(2)}, u32[]{:S(2)}) collective-permute-start(bf16[256,512]{1,0:T(8,128)(2,1)} %get-tuple-element.31), channel_id=1, source_target_pairs={{0,1},{1,0},{2,3},{3,2},{4,5},{5,4},{6,7},{7,6},{8,9},{9,8},{10,11... | collective-permute-start | bytes 786440 | tf_op jit(solution)/shard_map/ppermute | solution.py:184
  53.3 5.6 %partial_sums.11 = f32[3,256,512]{2,1,0:T(8,128)S(1)} custom-call(s32[3]{0:T(128)S(1)} %stack.47.place_ref, bf16[256,4800]{1,0:T(8,128)(2,1)S(1)} %normalize_templates.1.tpl_ref, bf16[3,24,2304]{2,1,0:T(8,128)(2,1)S(1)} %get-tuple-element.21.seg_ref, f32[3,24,2048]{2,1,0:T(8,128)S(1)} %get-tuple-element.22.scale_ref, bf16[256,512]{1,0:T(8,128)(2,1)} %get-tuple-element.29.refs_0_), custom_call_target="tpu_custom_call" | custom-call | flops 999999995904 | bytes 10000000000 | tf_op jit(solution)/shard_map/partial_sums/pallas_call | solution.py:139
  58.9 1.6 %collective-permute-done.10 = bf16[256,512]{1,0:T(8,128)(2,1)} collective-permute-done((bf16[256,512]{1,0:T(8,128)(2,1)}, bf16[256,512]{1,0:T(8,128)(2,1)}, u32[]{:S(2)}, u32[]{:S(2)}) %collective-permute-start.10) | collective-permute-done | bytes 262176 | tf_op jit(solution)/shard_map/ppermute | solution.py:184
  60.5 2.8 %collective-permute-done.9 = bf16[256,512]{1,0:T(8,128)(2,1)} collective-permute-done((bf16[256,512]{1,0:T(8,128)(2,1)}, bf16[256,512]{1,0:T(8,128)(2,1)}, u32[]{:S(2)}, u32[]{:S(2)}) %collective-permute-start.9) | collective-permute-done | bytes 262176 | tf_op jit(solution)/shard_map/ppermute | solution.py:184
  63.3 2.8 %select_bitcast_fusion = f32[256,3,512]{2,0,1:T(8,128)} fusion(f32[3,256,512]{2,1,0:T(8,128)S(1)} %partial_sums.11, bf16[1,256,512]{2,1,0:T(8,128)(2,1)} %bitcast.7, bf16[1,256,512]{2,1,0:T(8,128)(2,1)} %bitcast.6, bf16[1,256,512]{2,1,0:T(8,128)(2,1)} %bitcast.5, bf16[1,256,512]{2,1,0:T(8,128)(2,1)} %bitcast.10, bf16[1,256,512]{2,1,0:T(8,128)(2,1)} %bitcast.9, ...), kind=kLoop, calls=%fused_computation | loop fusion | flops 3538944 | bytes 4718848 | tf_op jit(solution)/shard_map/transpose | solution.py:262
  (19 shorter events, 0.0 us)
Async XLA Ops:
  0.0 8.9 %collective-permute-start = (bf16[1,24,2304]{2,1,0:T(8,128)(2,1)}, bf16[1,24,2304]{2,1,0:T(8,128)(2,1)S(1)}, u32[]{:S(2)}, u32[]{:S(2)}) collective-permute-start(bf16[1,24,2304]{2,1,0:T(8,128)(2,1)} %param.4), channel_id=1, source_target_pairs={{0,8},{4,12},{8,0},{12,4},{16,24},{20,28},{24,16},{28,20},{1,9},{5... | collective-permute-start | bytes 331784 | tf_op jit(solution)/shard_map/ppermute | solution.py:249
  3.0 11.6 %collective-permute-start.1 = (bf16[1,24,2304]{2,1,0:T(8,128)(2,1)}, bf16[1,24,2304]{2,1,0:T(8,128)(2,1)S(1)}, u32[]{:S(2)}, u32[]{:S(2)}) collective-permute-start(bf16[1,24,2304]{2,1,0:T(8,128)(2,1)} %param.4), channel_id=1, source_target_pairs={{0,16},{4,20},{8,24},{12,28},{16,0},{20,4},{24,8},{28,12},{1,17},{... | collective-permute-start | bytes 331784 | tf_op jit(solution)/shard_map/ppermute | solution.py:249
  5.6 9.0 %collective-permute-start.2 = (bf16[1,24,2304]{2,1,0:T(8,128)(2,1)}, bf16[1,24,2304]{2,1,0:T(8,128)(2,1)S(1)}, u32[]{:S(2)}, u32[]{:S(2)}) collective-permute-start(bf16[1,24,2304]{2,1,0:T(8,128)(2,1)} %param.4), channel_id=1, source_target_pairs={{0,24},{4,28},{8,16},{12,20},{16,8},{20,12},{24,0},{28,4},{1,25},{... | collective-permute-start | bytes 331784 | tf_op jit(solution)/shard_map/ppermute | solution.py:249
  5.6 1.7 %copy-start = (bf16[256,24,200]{0,2,1:T(8,128)(2,1)S(1)}, bf16[256,24,200]{0,2,1:T(8,128)(2,1)}, u32[]{:S(2)}) copy-start(bf16[256,24,200]{0,2,1:T(8,128)(2,1)} %param.5) | copy-start | bytes 7372804
  7.3 7.3 %copy-start.1 = (bf16[1,24,2304]{2,1,0:T(8,128)(2,1)S(1)}, bf16[1,24,2304]{2,1,0:T(8,128)(2,1)}, u32[]{:S(2)}) copy-start(bf16[1,24,2304]{2,1,0:T(8,128)(2,1)} %param.4) | copy-start | bytes 331780
  7.3 8.1 %copy-start.3 = (s32[3]{0:T(128)S(1)}, s32[3]{0:T(128)}, u32[]{:S(2)}) copy-start(s32[3]{0:T(128)} %param.7) | copy-start | bytes 40
  14.7 1.9 %collective-permute-start.3 = (bf16[4,24,2304]{2,1,0:T(8,128)(2,1)S(1)}, bf16[4,24,2304]{2,1,0:T(8,128)(2,1)S(1)}, u32[]{:S(2)}, u32[]{:S(2)}) collective-permute-start(bf16[4,24,2304]{2,1,0:T(8,128)(2,1)S(1)} %pad_maximum_fusion.even_ref), channel_id=1, source_target_pairs={{0,4},{4,0},{8,12},{12,8},{16,20},{20,16},{24,28},{28,24},{1,5},{5... | collective-permute-start | bytes 1327112 | tf_op jit(solution)/shard_map/ppermute | solution.py:252
  21.4 8.9 %collective-permute-start.4 = (bf16[1,128,512]{2,1,0:T(8,128)(2,1)}, bf16[1,128,512]{2,1,0:T(8,128)(2,1)}, u32[]{:S(2)}, u32[]{:S(2)}) collective-permute-start(bf16[1,128,512]{2,1,0:T(8,128)(2,1)} %get-tuple-element.23.refs_0_), channel_id=1, source_target_pairs={{0,2},{1,3},{2,0},{3,1},{4,6},{5,7},{6,4},{7,5},{8,10},{9,11},{10,... | collective-permute-start | bytes 393224 | tf_op jit(solution)/shard_map/ppermute | solution.py:184
  23.0 7.3 %collective-permute-start.5 = (bf16[1,128,512]{2,1,0:T(8,128)(2,1)}, bf16[1,128,512]{2,1,0:T(8,128)(2,1)}, u32[]{:S(2)}, u32[]{:S(2)}) collective-permute-start(bf16[1,128,512]{2,1,0:T(8,128)(2,1)} %get-tuple-element.25), channel_id=1, source_target_pairs={{0,1},{1,0},{2,3},{3,2},{4,5},{5,4},{6,7},{7,6},{8,9},{9,8},{10,11... | collective-permute-start | bytes 393224 | tf_op jit(solution)/shard_map/ppermute | solution.py:184
  29.3 9.3 %collective-permute-start.6 = (bf16[2,128,512]{2,1,0:T(8,128)(2,1)}, bf16[2,128,512]{2,1,0:T(8,128)(2,1)}, u32[]{:S(2)}, u32[]{:S(2)}) collective-permute-start(bf16[2,128,512]{2,1,0:T(8,128)(2,1)} %get-tuple-element.24.refs_0_), channel_id=1, source_target_pairs={{0,2},{1,3},{2,0},{3,1},{4,6},{5,7},{6,4},{7,5},{8,10},{9,11},{10,... | collective-permute-start | bytes 786440 | tf_op jit(solution)/shard_map/ppermute | solution.py:184
  29.8 8.8 %collective-permute-start.7 = (bf16[2,128,512]{2,1,0:T(8,128)(2,1)}, bf16[2,128,512]{2,1,0:T(8,128)(2,1)}, u32[]{:S(2)}, u32[]{:S(2)}) collective-permute-start(bf16[2,128,512]{2,1,0:T(8,128)(2,1)} %get-tuple-element.27), channel_id=1, source_target_pairs={{0,1},{1,0},{2,3},{3,2},{4,5},{5,4},{6,7},{7,6},{8,9},{9,8},{10,11... | collective-permute-start | bytes 786440 | tf_op jit(solution)/shard_map/ppermute | solution.py:184
  35.5 16.3 %collective-permute-start.8 = (bf16[256,512]{1,0:T(8,128)(2,1)}, bf16[256,512]{1,0:T(8,128)(2,1)}, u32[]{:S(2)}, u32[]{:S(2)}) collective-permute-start(bf16[256,512]{1,0:T(8,128)(2,1)} %get-tuple-element.30), channel_id=1, source_target_pairs={{0,1},{1,0},{2,3},{3,2},{4,5},{5,4},{6,7},{7,6},{8,9},{9,8},{10,11... | collective-permute-start | bytes 786440 | tf_op jit(solution)/shard_map/ppermute | solution.py:184
  37.0 21.9 %collective-permute-start.11 = (bf16[256,512]{1,0:T(8,128)(2,1)}, bf16[256,512]{1,0:T(8,128)(2,1)}, u32[]{:S(2)}, u32[]{:S(2)}) collective-permute-start(bf16[256,512]{1,0:T(8,128)(2,1)} %get-tuple-element.26.refs_0_), channel_id=1, source_target_pairs={{0,2},{1,3},{2,0},{3,1},{4,6},{5,7},{6,4},{7,5},{8,10},{9,11},{10,... | collective-permute-start | bytes 786440 | tf_op jit(solution)/shard_map/ppermute | solution.py:184
  44.0 19.3 %collective-permute-start.12 = (bf16[256,512]{1,0:T(8,128)(2,1)}, bf16[256,512]{1,0:T(8,128)(2,1)}, u32[]{:S(2)}, u32[]{:S(2)}) collective-permute-start(bf16[256,512]{1,0:T(8,128)(2,1)} %get-tuple-element.28.refs_0_), channel_id=1, source_target_pairs={{0,2},{1,3},{2,0},{3,1},{4,6},{5,7},{6,4},{7,5},{8,10},{9,11},{10,... | collective-permute-start | bytes 786440 | tf_op jit(solution)/shard_map/ppermute | solution.py:184
  50.0 9.0 %collective-permute-start.13 = (bf16[256,512]{1,0:T(8,128)(2,1)}, bf16[256,512]{1,0:T(8,128)(2,1)}, u32[]{:S(2)}, u32[]{:S(2)}) collective-permute-start(bf16[256,512]{1,0:T(8,128)(2,1)} %get-tuple-element.29.refs_0_), channel_id=1, source_target_pairs={{0,2},{1,3},{2,0},{3,1},{4,6},{5,7},{6,4},{7,5},{8,10},{9,11},{10,... | collective-permute-start | bytes 786440 | tf_op jit(solution)/shard_map/ppermute | solution.py:184
  51.3 9.2 %collective-permute-start.10 = (bf16[256,512]{1,0:T(8,128)(2,1)}, bf16[256,512]{1,0:T(8,128)(2,1)}, u32[]{:S(2)}, u32[]{:S(2)}) collective-permute-start(bf16[256,512]{1,0:T(8,128)(2,1)} %get-tuple-element.32), channel_id=1, source_target_pairs={{0,1},{1,0},{2,3},{3,2},{4,5},{5,4},{6,7},{7,6},{8,9},{9,8},{10,11... | collective-permute-start | bytes 786440 | tf_op jit(solution)/shard_map/ppermute | solution.py:184
  51.8 11.5 %collective-permute-start.9 = (bf16[256,512]{1,0:T(8,128)(2,1)}, bf16[256,512]{1,0:T(8,128)(2,1)}, u32[]{:S(2)}, u32[]{:S(2)}) collective-permute-start(bf16[256,512]{1,0:T(8,128)(2,1)} %get-tuple-element.31), channel_id=1, source_target_pairs={{0,1},{1,0},{2,3},{3,2},{4,5},{5,4},{6,7},{7,6},{8,9},{9,8},{10,11... | collective-permute-start | bytes 786440 | tf_op jit(solution)/shard_map/ppermute | solution.py:184
  53.3 10.0 %copy-start.2 = (pred[256]{0:T(512)(128)(4,1)S(1)}, pred[256]{0:T(512)(128)(4,1)}, u32[]{:S(2)}) copy-start(pred[256]{0:T(512)(128)(4,1)} %iota_compare_fusion) | copy-start | bytes 772
where the time goes:
time: 66.3 us; the launch traced here: 66.1 us
  Pallas kernels  32 us (48%)
  starting transfers between devices  16.9 us (25%)
  waiting for transfers between devices  11.2 us (17%)
  other arithmetic  3.55 us (5%)
  local copies, waits for them, and re-layouts  1.71 us (3%)
  between operations  0.73 us (1%)
    pallas_call x6, Pallas kernels, partial_sums(): pl.pallas_call(functools.partial(partial_kernel, chunks, len(adds), write...  28.9 us
    ppermute x10, starting transfers between devices, exchange(): return lax.ppermute(value, 'chan', [(i, i ^ step) for i in range(n_chan)])  11.2 us
    ppermute x3, waiting for transfers between devices, body(): lax.ppermute(data, 'tmpl', [(i, i ^ step) for i in range(n_tmpl)])  5.72 us
    ppermute x3, starting transfers between devices, body(): lax.ppermute(data, 'tmpl', [(i, i ^ step) for i in range(n_tmpl)])  5.62 us
    ppermute x10, waiting for transfers between devices, exchange(): return lax.ppermute(value, 'chan', [(i, i ^ step) for i in range(n_chan)])  4.4 us
    transpose x1, other arithmetic, body(): return jnp.transpose(jnp.where(live, total, 0.0), (1, 0, 2))  2.76 us
    pallas_call x1, Pallas kernels, choose_blocks(): pl.pallas_call(block_kernel, out_shape=(jax.ShapeDtypeStruct((NB, held, l...  2.31 us
    unnamed x8, local copies, waits for them, and re-layouts  1.7 us
  transfers between devices with their start and end apart: 14, of which 4 were waited for; matrix products, arithmetic and copies ran while one was open for 1% of the time, Pallas kernels for 41%

commit v1 on v0

--- a/solution.py
+++ b/solution.py
@@ -20,14 +20,15 @@
     return 1.0 / (jnp.sqrt(mean_square + EPS) * math.sqrt(W))
 
 
-def template_kernel(tpl_ref, out_ref, scaled_ref):
+def template_kernel(count_ref, tpl_ref, out_ref, scaled_ref):
     chans, _, slots = tpl_ref.shape
+    live = lax.broadcasted_iota(jnp.int32, (1, slots), 1) < count_ref[0]
     for c in range(0, chans, 2):
         pair = []
         for k in (c, c + 1):
             values = tpl_ref[k].astype(jnp.float32)
             mean_square = jnp.sum(values * values, axis=0, keepdims=True) * (1.0 / W)
-            pair.append(values * inverse_norm(mean_square))
+            pair.append(jnp.where(live, values * inverse_norm(mean_square), 0.0))
         scaled_ref[c * W : (c + 2) * W, :] = jnp.concatenate(pair, 0).astype(jnp.bfloat16)
     depth = chans * W
     for at in range(0, depth, slots):
@@ -35,18 +36,22 @@
         out_ref[:, at : at + size] = scaled_ref[at : at + size, :].T
 
 
-def normalize_templates(templates):
+def normalize_templates(counts, templates):
     slots, chans, _ = templates.shape
     return pl.pallas_call(
         template_kernel,
         out_shape=jax.ShapeDtypeStruct((slots, chans * W), jnp.bfloat16),
+        in_specs=[
+            pl.BlockSpec(memory_space=pltpu.SMEM),
+            pl.BlockSpec(memory_space=pltpu.VMEM),
+        ],
         scratch_shapes=[pltpu.VMEM((chans * W, slots), jnp.bfloat16)],
         compiler_params=pltpu.CompilerParams(vmem_limit_bytes=VMEM_LIMIT),
         cost_estimate=pl.CostEstimate(
             flops=4 * slots * chans * W, bytes_accessed=4 * slots * chans * W, transcendentals=0
         ),
         name="normalize_templates",
-    )(jnp.transpose(templates, (1, 2, 0)))
+    )(counts, jnp.transpose(templates, (1, 2, 0)))
 
 
 def shift_left(x, amount):
@@ -108,8 +113,8 @@
         win_ref[c * W : (c + 2) * W, :] = jnp.concatenate(rows, 0).astype(jnp.bfloat16)
 
 
-def partial_kernel(chunks, n_add, write, place_ref, tpl_ref, seg_ref, scale_ref, *refs):
-    adds, outs = refs[1 : 1 + n_add], refs[1 + n_add : -4]
+def partial_kernel(chunks, n_add, n_order, write, place_ref, tpl_ref, seg_ref, scale_ref, *refs):
+    adds, outs = refs[:n_add], refs[n_add + n_order : -4]
     seg_now, scale_now, base_now, win_ref = refs[-4:]
     depth, lags = win_ref.shape
     held = seg_ref.shape[1]
@@ -130,23 +135,22 @@
         write(index, product, adds, outs)
 
 
-def partial_sums(chunks, write, outs, place, normed, segments, scales, adds=(), order=None):
+def partial_sums(chunks, write, outs, place, normed, segments, scales, adds=(), order=()):
     lags = outs[0].shape[-1]
     depth = normed.shape[1]
     held = segments.shape[1]
     whole = pl.BlockSpec(memory_space=pltpu.VMEM)
-    order = place if order is None else order
     return pl.pallas_call(
-        functools.partial(partial_kernel, chunks, len(adds), write),
+        functools.partial(partial_kernel, chunks, len(adds), len(order), write),
         out_shape=outs,
         in_specs=[
             pl.BlockSpec(memory_space=pltpu.SMEM),
             whole,
             whole,
             whole,
-            pl.BlockSpec(memory_space=pl.ANY),
         ]
-        + [whole] * len(adds),
+        + [whole] * len(adds)
+        + [pl.BlockSpec(memory_space=pl.ANY)] * len(order),
         scratch_shapes=[
             pltpu.VMEM((len(chunks) * held, lags + 256), jnp.float32),
             pltpu.VMEM((len(chunks) * held, lags), jnp.float32),
@@ -156,17 +160,23 @@
         compiler_params=pltpu.CompilerParams(vmem_limit_bytes=VMEM_LIMIT),
         cost_estimate=pl.CostEstimate(flops=10**12, bytes_accessed=10**10, transcendentals=0),
         name="partial_sums",
-    )(place, normed, segments, scales, order, *adds)
+    )(place, normed, segments, scales, *adds, *order)
 
 
 def write_plain(index, product, adds, outs):
-    outs[0][index] = product.astype(outs[0].dtype)
-
-
-def write_halves(index, product, adds, outs):
+    if len(outs) == 1:
+        outs[0][index] = product.astype(outs[0].dtype)
+    else:
+        outs[index][...] = product.astype(outs[index].dtype)
+
+
+def write_across(index, product, adds, outs):
     half = outs[0].shape[1]
-    outs[0][index] = product[:half].astype(jnp.bfloat16)
-    outs[1][index] = product[half:].astype(jnp.bfloat16)
+    if index < outs[0].shape[0]:
+        outs[0][index] = product[:half].astype(jnp.bfloat16)
+        outs[1][index] = product[half:].astype(jnp.bfloat16)
+    else:
+        outs[2][...] = product.astype(jnp.bfloat16)
 
 
 def write_added(at, index, product, adds, outs):
@@ -189,39 +199,89 @@
     me = lax.axis_index("chan")
     args = (normed, segments, scales)
 
-    def message(count, rows):
-        return jax.ShapeDtypeStruct((count, rows, lags), jnp.bfloat16)
-
-    via_x, via_y = [], []
-    order = None
-    for chunks in ((0,), (1, 2)):
-        out = (message(len(chunks), slots // 2),) * 2
-        place = jnp.stack([me ^ 3] * len(chunks))
-        upper, lower = partial_sums(chunks, write_halves, out, place, *args, order=order)
-        order = lower
-        via_x.append(exchange(upper, 1, 4))
-        via_y.append(exchange(lower, 2, 4))
+    def message(*shape):
+        return jax.ShapeDtypeStruct(shape + (lags,), jnp.bfloat16)
+
+    upper, lower, far = partial_sums(
+        (1, 2, 0),
+        write_across,
+        (message(2, slots // 2), message(2, slots // 2), message(slots)),
+        jnp.stack([me ^ 3] * NB),
+        *args,
+    )
+    via_x, via_y = exchange(upper, 1, 4), exchange(lower, 2, 4)
+    straight = exchange(far, 3, 4)
     arrived = []
     place = jnp.stack([me ^ 1, me ^ 2])
+    order = (far,)
     for number in range(NB):
-        part, at = (0, 0) if number == 0 else (1, number - 1)
-        out = (jax.ShapeDtypeStruct((slots, lags), jnp.bfloat16),) * 2
+        write, adds = write_plain, ()
+        if number > 0:
+            write, adds = functools.partial(write_added, number - 1), (via_y, via_x)
         to_x, to_y = partial_sums(
-            (number, number),
-            functools.partial(write_added, at),
-            out,
-            place,
-            *args,
-            adds=(via_y[part], via_x[part]),
-            order=order,
+            (number, number), write, (message(slots),) * 2, place, *args, adds=adds, order=order
         )
-        order = to_y
+        order = (to_y,)
+        if number == 1:
+            order += (straight,)
+        if number == NB - 1:
+            to_x, to_y, *first = lax.optimization_barrier((to_x, to_y, *arrived[0]))
+            arrived[0] = tuple(first)
         arrived.append((exchange(to_x, 1, 4), exchange(to_y, 2, 4)))
-    out = (jax.ShapeDtypeStruct((NB, slots, lags), jnp.float32),)
     (total,) = partial_sums(
-        tuple(range(NB)), write_plain, out, jnp.stack([me] * NB), *args, order=order
+        tuple(range(NB)),
+        write_plain,
+        (jax.ShapeDtypeStruct((NB, slots, lags), jnp.float32),),
+        jnp.stack([me] * NB),
+        *args,
+        order=order[:1],
     )
-    return total, [jnp.stack([pair[side] for pair in arrived]) for side in range(2)]
+    arrived[0] += (straight,)
+    return finish(total, arrived)
+
+
+def finish_kernel(shares, total_ref, *refs):
+    n_part = sum(shares)
+    parts, out_ref, stage = refs[:n_part], refs[n_part], refs[n_part + 1]
+    held = refs[n_part + 2 : 2 * n_part + 2]
+    semaphores = refs[2 * n_part + 2 :]
+    arriving = [pltpu.make_async_copy(*trio) for trio in zip(parts, held, semaphores)]
+    for copy in arriving:
+        copy.start()
+    leaving = []
+    at = 0
+    for number, share in enumerate(shares):
+        value = total_ref[number]
+        for index in range(at, at + share):
+            arriving[index].wait()
+            value = value + held[index][...].astype(jnp.float32)
+        at += share
+        stage[number] = value
+        leaving.append(
+            pltpu.make_async_copy(
+                stage.at[number], out_ref.at[number], semaphores[n_part + number]
+            )
+        )
+        leaving[number].start()
+    for copy in leaving:
+        copy.wait()
+
+
+def finish(total, arrived):
+    parts = [one for group in arrived for one in group]
+    anywhere = pl.BlockSpec(memory_space=pl.ANY)
+    return pl.pallas_call(
+        functools.partial(finish_kernel, [len(group) for group in arrived]),
+        out_shape=jax.ShapeDtypeStruct(total.shape, jnp.float32),
+        in_specs=[pl.BlockSpec(memory_space=pltpu.VMEM)] + [anywhere] * len(parts),
+        out_specs=anywhere,
+        scratch_shapes=[pltpu.VMEM(total.shape, jnp.float32)]
+        + [pltpu.VMEM(part.shape, part.dtype) for part in parts]
+        + [pltpu.SemaphoreType.DMA] * (len(parts) + total.shape[0]),
+        compiler_params=pltpu.CompilerParams(vmem_limit_bytes=VMEM_LIMIT),
+        cost_estimate=pl.CostEstimate(flops=10**9, bytes_accessed=10**7, transcendentals=0),
+        name="finish",
+    )(total, *parts)
 
 
 def one_step(normed, segments, scales, lags, n_chan):
@@ -229,17 +289,20 @@
     me = lax.axis_index("chan")
     every = tuple(range(NB))
     arrived = []
-    order = None
+    order = ()
     for step in range(n_chan - 1, -1, -1):
         dtype = jnp.bfloat16 if step else jnp.float32
         out = (jax.ShapeDtypeStruct((NB, slots, lags), dtype),)
         place = jnp.stack([me ^ step] * NB)
-        (order,) = partial_sums(
+        order = partial_sums(
             every, write_plain, out, place, normed, segments, scales, order=order
         )
         if step:
-            arrived.append(exchange(order, step, n_chan))
-    return order, arrived
+            arrived.append(exchange(order[0], step, n_chan))
+    total = order[0]
+    for part in arrived:
+        total = total + part.astype(jnp.float32)
+    return total
 
 
 def body(n_tmpl, n_chan, data, templates, counts, owners):
@@ -247,19 +310,16 @@
     parts = [data]
     for step in range(2, n_tmpl, 2):
         parts.append(lax.ppermute(data, "tmpl", [(i, i ^ step) for i in range(n_tmpl)]))
-    normed = normalize_templates(templates)
+    normed = normalize_templates(counts, templates)
     even, normed = lax.optimization_barrier((jnp.concatenate(parts, 0), normed))
     odd = lax.ppermute(even, "tmpl", [(i, i ^ 1) for i in range(n_tmpl)])
     codes = owners ^ lax.axis_index("tmpl")
     segments, scales = choose_blocks(codes, even, odd)
     if n_chan == 4:
-        total, arrived = two_steps(normed, segments, scales, lags)
+        total = two_steps(normed, segments, scales, lags)
     else:
-        total, arrived = one_step(normed, segments, scales, lags, n_chan)
-    for part in arrived:
-        total = total + part.astype(jnp.float32)
-    live = lax.broadcasted_iota(jnp.int32, total.shape, 1) < counts[0]
-    return jnp.transpose(jnp.where(live, total, 0.0), (1, 0, 2))
+        total = one_step(normed, segments, scales, lags, n_chan)
+    return jnp.transpose(total, (1, 0, 2))
 
 
 def solution(mesh):

time: 66.3 us -> 61.7 us (0.931)
  other arithmetic: 3.55 us -> 0.14 us
  waiting for transfers between devices: 11.2 us -> 9.7 us
  Pallas kernels: 32 us -> 32.8 us
    transpose x1 -> x0, other arithmetic: 2.76 us -> none  [body(): return jnp.transpose(jnp.where(live, total, 0.0), (1, 0, 2))]
    ppermute x3, waiting for transfers between devices: 5.72 us -> 4.24 us  [body(): lax.ppermute(data, 'tmpl', [(i, i ^ step) for i in range(n_tmpl)])]
    ppermute x10 -> x9, waiting for transfers between devices: 4.4 us -> 3.77 us  [exchange(): return lax.ppermute(value, 'chan', [(i, i ^ step) for i in range(n_chan)])]
    ppermute x10 -> x9, starting transfers between devices: 11.2 us -> 10.6 us  [exchange(): return lax.ppermute(value, 'chan', [(i, i ^ step) for i in range(n_chan)])]
    unnamed x8 -> x6, local copies, waits for them, and re-layouts: 1.7 us -> 1.69 us
  transfers between devices with their start and end apart: 14 -> 13, of which waited for: 4 -> 6; matrix products, arithmetic and copies ran while one was open for 1% -> 0% of each run, Pallas kernels for 41% -> 35%
where the time goes in v1:
time: 61.7 us; the launch traced here: 61.5 us
  Pallas kernels  32.8 us (53%)
  starting transfers between devices  16.3 us (26%)
  waiting for transfers between devices  9.7 us (16%)
  local copies, waits for them, and re-layouts  1.7 us (3%)
  between operations  0.89 us (1%)
    pallas_call x5, Pallas kernels, partial_sums(): pl.pallas_call(functools.partial(partial_kernel, chunks, len(adds), len(o...  27 us
    ppermute x9, starting transfers between devices, exchange(): return lax.ppermute(value, 'chan', [(i, i ^ step) for i in range(n_chan)])  10.6 us
    ppermute x3, starting transfers between devices, body(): lax.ppermute(data, 'tmpl', [(i, i ^ step) for i in range(n_tmpl)])  5.62 us
    ppermute x3, waiting for transfers between devices, body(): lax.ppermute(data, 'tmpl', [(i, i ^ step) for i in range(n_tmpl)])  4.24 us
    ppermute x9, waiting for transfers between devices, exchange(): return lax.ppermute(value, 'chan', [(i, i ^ step) for i in range(n_chan)])  3.77 us
    pallas_call x1, Pallas kernels, finish(): pl.pallas_call(functools.partial(finish_kernel, [len(group) for group in...  2.41 us
    pallas_call x1, Pallas kernels, choose_blocks(): pl.pallas_call(block_kernel, out_shape=(jax.ShapeDtypeStruct((NB, held, l...  2.31 us
    unnamed x6, local copies, waits for them, and re-layouts  1.69 us
  transfers between devices with their start and end apart: 13, of which 6 were waited for; matrix products, arithmetic and copies ran while one was open for 0% of the time, Pallas kernels for 35%

profile of v1, /device:TPU:0, one launch (start us, length us, event | category | flops | bytes accessed | tf_op | source)
XLA Modules:
  0.0 61.5 jit_solution(3987227996882857663)
XLA Ops:
  0.0 4.0 %collective-permute-start.1 = (bf16[1,24,2304]{2,1,0:T(8,128)(2,1)}, bf16[1,24,2304]{2,1,0:T(8,128)(2,1)S(1)}, u32[]{:S(2)}, u32[]{:S(2)}) collective-permute-start(bf16[1,24,2304]{2,1,0:T(8,128)(2,1)} %param.4), channel_id=1, source_target_pairs={{0,16},{4,20},{8,24},{12,28},{16,0},{20,4},{24,8},{28,12},{1,17},{... | collective-permute-start | bytes 331784 | tf_op jit(solution)/shard_map/ppermute | solution.py:312
  4.0 1.6 %collective-permute-start = (bf16[1,24,2304]{2,1,0:T(8,128)(2,1)}, bf16[1,24,2304]{2,1,0:T(8,128)(2,1)S(1)}, u32[]{:S(2)}, u32[]{:S(2)}) collective-permute-start(bf16[1,24,2304]{2,1,0:T(8,128)(2,1)} %param.4), channel_id=1, source_target_pairs={{0,8},{4,12},{8,0},{12,4},{16,24},{20,28},{24,16},{28,20},{1,9},{5... | collective-permute-start | bytes 331784 | tf_op jit(solution)/shard_map/ppermute | solution.py:312
  5.6 0.0 collective-permute-start.2
  6.3 1.7 %copy-done = bf16[256,24,200]{0,2,1:T(8,128)(2,1)S(1)} copy-done((bf16[256,24,200]{0,2,1:T(8,128)(2,1)S(1)}, bf16[256,24,200]{0,2,1:T(8,128)(2,1)}, u32[]{:S(2)}) %copy-start) | copy-done | bytes 2457624
  8.0 1.0 %normalize_templates.1.tpl_ref = bf16[256,4800]{1,0:T(8,128)(2,1)S(1)} custom-call(s32[1]{0:T(128)S(6)} %copy.5.count_ref, bf16[24,200,256]{2,1,0:T(8,128)(2,1)S(1)} %bitcast.4), custom_call_target="tpu_custom_call" | custom-call | flops 4915200 | bytes 4915200 | tf_op jit(solution)/shard_map/normalize_templates/pallas_call | solution.py:41
  9.0 2.3 %collective-permute-done.1 = bf16[1,24,2304]{2,1,0:T(8,128)(2,1)S(1)} collective-permute-done((bf16[1,24,2304]{2,1,0:T(8,128)(2,1)}, bf16[1,24,2304]{2,1,0:T(8,128)(2,1)S(1)}, u32[]{:S(2)}, u32[]{:S(2)}) %collective-permute-start.1) | collective-permute-done | bytes 110624 | tf_op jit(solution)/shard_map/ppermute | solution.py:312
  11.3 1.9 %collective-permute-done.2 = bf16[1,24,2304]{2,1,0:T(8,128)(2,1)S(1)} collective-permute-done((bf16[1,24,2304]{2,1,0:T(8,128)(2,1)}, bf16[1,24,2304]{2,1,0:T(8,128)(2,1)S(1)}, u32[]{:S(2)}, u32[]{:S(2)}) %collective-permute-start.2) | collective-permute-done | bytes 110624 | tf_op jit(solution)/shard_map/ppermute | solution.py:312
  13.2 0.1 pad_maximum_fusion.even_ref
  13.3 0.1 collective-permute-start.3
  13.4 0.1 pad_add_fusion.place_ref
  13.4 1.7 %collective-permute-done.3.odd_ref = bf16[4,24,2304]{2,1,0:T(8,128)(2,1)S(1)} collective-permute-done((bf16[4,24,2304]{2,1,0:T(8,128)(2,1)S(1)}, bf16[4,24,2304]{2,1,0:T(8,128)(2,1)S(1)}, u32[]{:S(2)}, u32[]{:S(2)}) %collective-permute-start.3) | collective-permute-done | bytes 442400 | tf_op jit(solution)/shard_map/ppermute | solution.py:315
  15.1 2.3 %choose_blocks.1 = (bf16[3,24,2304]{2,1,0:T(8,128)(2,1)S(1)}, f32[3,24,2048]{2,1,0:T(8,128)S(1)}) custom-call(s32[3]{0:T(128)S(1)} %broadcast_xor_fusion.code_ref, bf16[4,24,2304]{2,1,0:T(8,128)(2,1)S(1)} %pad_maximum_fusion.even_ref, bf16[4,24,2304]{2,1,0:T(8,128)(2,1)S(1)} %collective-permute-done.3.odd_ref), custom_call_target="tpu_custom_call" | custom-call | flops 10000000000 | bytes 100000000 | tf_op jit(solution)/shard_map/choose_blocks/pallas_call | solution.py:83
  17.5 6.2 %partial_sums.5 = (bf16[2,128,512]{2,1,0:T(8,128)(2,1)}, bf16[2,128,512]{2,1,0:T(8,128)(2,1)}, bf16[256,512]{1,0:T(8,128)(2,1)}) custom-call(s32[3]{0:T(128)S(1)} %stack.25.place_ref, bf16[256,4800]{1,0:T(8,128)(2,1)S(1)} %normalize_templates.1.tpl_ref, bf16[3,24,2304]{2,1,0:T(8,128)(2,1)S(1)} %get-tuple-element.24.seg_ref, ...), custom_call_target="tpu_custom_call" | custom-call | flops 999999995904 | bytes 10000000000 | tf_op jit(solution)/shard_map/partial_sums/pallas_call | solution.py:143
  23.7 1.5 %collective-permute-start.4 = (bf16[2,128,512]{2,1,0:T(8,128)(2,1)}, bf16[2,128,512]{2,1,0:T(8,128)(2,1)}, u32[]{:S(2)}, u32[]{:S(2)}) collective-permute-start(bf16[2,128,512]{2,1,0:T(8,128)(2,1)} %get-tuple-element.26), channel_id=1, source_target_pairs={{0,2},{1,3},{2,0},{3,1},{4,6},{5,7},{6,4},{7,5},{8,10},{9,11},{10,... | collective-permute-start | bytes 786440 | tf_op jit(solution)/shard_map/ppermute | solution.py:194
  25.2 1.5 %collective-permute-start.5 = (bf16[2,128,512]{2,1,0:T(8,128)(2,1)}, bf16[2,128,512]{2,1,0:T(8,128)(2,1)}, u32[]{:S(2)}, u32[]{:S(2)}) collective-permute-start(bf16[2,128,512]{2,1,0:T(8,128)(2,1)} %get-tuple-element.27), channel_id=1, source_target_pairs={{0,1},{1,0},{2,3},{3,2},{4,5},{5,4},{6,7},{7,6},{8,9},{9,8},{10,11... | collective-permute-start | bytes 786440 | tf_op jit(solution)/shard_map/ppermute | solution.py:194
  26.7 0.5 collective-permute-start.6
  27.2 4.7 %partial_sums.6 = (bf16[256,512]{1,0:T(8,128)(2,1)}, bf16[256,512]{1,0:T(8,128)(2,1)}) custom-call(s32[2]{0:T(128)S(1)} %pad_add_fusion.place_ref, bf16[256,4800]{1,0:T(8,128)(2,1)S(1)} %normalize_templates.1.tpl_ref, bf16[3,24,2304]{2,1,0:T(8,128)(2,1)S(1)} %get-tuple-element.24.seg_ref, f32[3,24,2048]{2,1,0:T(8,128)S(1)} %get-tuple-element.25.scale_ref, ...), custom_call_target="tpu_custom_call" | custom-call | flops 999999995904 | bytes 10000000000 | tf_op jit(solution)/shard_map/partial_sums/pallas_call | solution.py:143
  31.9 1.5 %collective-permute-start.7 = (bf16[256,512]{1,0:T(8,128)(2,1)}, bf16[256,512]{1,0:T(8,128)(2,1)}, u32[]{:S(2)}, u32[]{:S(2)}) collective-permute-start(bf16[256,512]{1,0:T(8,128)(2,1)} %get-tuple-element.33), channel_id=1, source_target_pairs={{0,1},{1,0},{2,3},{3,2},{4,5},{5,4},{6,7},{7,6},{8,9},{9,8},{10,11... | collective-permute-start | bytes 786440 | tf_op jit(solution)/shard_map/ppermute | solution.py:194
  33.4 1.5 %collective-permute-start.8 = (bf16[256,512]{1,0:T(8,128)(2,1)}, bf16[256,512]{1,0:T(8,128)(2,1)}, u32[]{:S(2)}, u32[]{:S(2)}) collective-permute-start(bf16[256,512]{1,0:T(8,128)(2,1)} %get-tuple-element.29.refs_2_), channel_id=1, source_target_pairs={{0,2},{1,3},{2,0},{3,1},{4,6},{5,7},{6,4},{7,5},{8,10},{9,11},{10,... | collective-permute-start | bytes 786440 | tf_op jit(solution)/shard_map/ppermute | solution.py:194
  34.9 0.0 collective-permute-done.4.refs_0_
  34.9 5.4 %partial_sums.7 = (bf16[256,512]{1,0:T(8,128)(2,1)}, bf16[256,512]{1,0:T(8,128)(2,1)}) custom-call(s32[2]{0:T(128)S(1)} %pad_add_fusion.place_ref, bf16[256,4800]{1,0:T(8,128)(2,1)S(1)} %normalize_templates.1.tpl_ref, bf16[3,24,2304]{2,1,0:T(8,128)(2,1)S(1)} %get-tuple-element.24.seg_ref, f32[3,24,2048]{2,1,0:T(8,128)S(1)} %get-tuple-element.25.scale_ref, ...), custom_call_target="tpu_custom_call" | custom-call | flops 999999995904 | bytes 10000000000 | tf_op jit(solution)/shard_map/partial_sums/pallas_call | solution.py:143
  40.3 0.5 collective-permute-start.10
  40.8 0.0 collective-permute-done.6.refs_3_.refs_2_
  40.8 5.2 %partial_sums.8 = (bf16[256,512]{1,0:T(8,128)(2,1)}, bf16[256,512]{1,0:T(8,128)(2,1)}) custom-call(s32[2]{0:T(128)S(1)} %pad_add_fusion.place_ref, bf16[256,4800]{1,0:T(8,128)(2,1)S(1)} %normalize_templates.1.tpl_ref, bf16[3,24,2304]{2,1,0:T(8,128)(2,1)S(1)} %get-tuple-element.24.seg_ref, f32[3,24,2048]{2,1,0:T(8,128)S(1)} %get-tuple-element.25.scale_ref, ...), custom_call_target="tpu_custom_call" | custom-call | flops 999999995904 | bytes 10000000000 | tf_op jit(solution)/shard_map/partial_sums/pallas_call | solution.py:143
  46.0 1.4 %collective-permute-start.11 = (bf16[256,512]{1,0:T(8,128)(2,1)}, bf16[256,512]{1,0:T(8,128)(2,1)}, u32[]{:S(2)}, u32[]{:S(2)}) collective-permute-start(bf16[256,512]{1,0:T(8,128)(2,1)} %get-tuple-element.37), channel_id=1, source_target_pairs={{0,1},{1,0},{2,3},{3,2},{4,5},{5,4},{6,7},{7,6},{8,9},{9,8},{10,11... | collective-permute-start | bytes 786440 | tf_op jit(solution)/shard_map/ppermute | solution.py:194
  47.4 1.5 %collective-permute-start.12 = (bf16[256,512]{1,0:T(8,128)(2,1)}, bf16[256,512]{1,0:T(8,128)(2,1)}, u32[]{:S(2)}, u32[]{:S(2)}) collective-permute-start(bf16[256,512]{1,0:T(8,128)(2,1)} %get-tuple-element.38.refs_0_), channel_id=1, source_target_pairs={{0,2},{1,3},{2,0},{3,1},{4,6},{5,7},{6,4},{7,5},{8,10},{9,11},{10,... | collective-permute-start | bytes 786440 | tf_op jit(solution)/shard_map/ppermute | solution.py:194
  48.9 0.7 %collective-permute-start.9 = (bf16[256,512]{1,0:T(8,128)(2,1)}, bf16[256,512]{1,0:T(8,128)(2,1)}, u32[]{:S(2)}, u32[]{:S(2)}) collective-permute-start(bf16[256,512]{1,0:T(8,128)(2,1)} %get-tuple-element.36), channel_id=1, source_target_pairs={{0,1},{1,0},{2,3},{3,2},{4,5},{5,4},{6,7},{7,6},{8,9},{9,8},{10,11... | collective-permute-start | bytes 786440 | tf_op jit(solution)/shard_map/ppermute | solution.py:194
  49.6 5.5 %partial_sums.9.total_ref = f32[3,256,512]{2,1,0:T(8,128)S(1)} custom-call(s32[3]{0:T(128)S(1)} %stack.10.place_ref, bf16[256,4800]{1,0:T(8,128)(2,1)S(1)} %normalize_templates.1.tpl_ref, bf16[3,24,2304]{2,1,0:T(8,128)(2,1)S(1)} %get-tuple-element.24.seg_ref, f32[3,24,2048]{2,1,0:T(8,128)S(1)} %get-tuple-element.25.scale_ref, ...), custom_call_target="tpu_custom_call" | custom-call | flops 999999995904 | bytes 10000000000 | tf_op jit(solution)/shard_map/partial_sums/pallas_call | solution.py:143
  55.2 0.5 collective-permute-done.11.refs_5_
  55.7 0.3 collective-permute-done.12.refs_6_
  56.0 2.9 %collective-permute-done.9.refs_3_ = bf16[256,512]{1,0:T(8,128)(2,1)} collective-permute-done((bf16[256,512]{1,0:T(8,128)(2,1)}, bf16[256,512]{1,0:T(8,128)(2,1)}, u32[]{:S(2)}, u32[]{:S(2)}) %collective-permute-start.9) | collective-permute-done | bytes 262176 | tf_op jit(solution)/shard_map/ppermute | solution.py:194
  58.9 2.4 %finish.1 = f32[3,256,512]{2,1,0:T(8,128)} custom-call(f32[3,256,512]{2,1,0:T(8,128)S(1)} %partial_sums.9.total_ref, bf16[256,512]{1,0:T(8,128)(2,1)} %collective-permute-done.7.refs_0_, bf16[256,512]{1,0:T(8,128)(2,1)} %collective-permute-done.8.refs_1_, bf16[256,512]{1,0:T(8,128)(2,1)} %collective-permute-done.6.refs_3_.refs_2_, ...), custom_call_target="tpu_custom_call" | custom-call | flops 1000000000 | bytes 10000000 | tf_op jit(solution)/shard_map/finish/pallas_call | solution.py:273
  (13 shorter events, 0.0 us)
Async XLA Ops:
  0.0 11.3 %collective-permute-start.1 = (bf16[1,24,2304]{2,1,0:T(8,128)(2,1)}, bf16[1,24,2304]{2,1,0:T(8,128)(2,1)S(1)}, u32[]{:S(2)}, u32[]{:S(2)}) collective-permute-start(bf16[1,24,2304]{2,1,0:T(8,128)(2,1)} %param.4), channel_id=1, source_target_pairs={{0,16},{4,20},{8,24},{12,28},{16,0},{20,4},{24,8},{28,12},{1,17},{... | collective-permute-start | bytes 331784 | tf_op jit(solution)/shard_map/ppermute | solution.py:312
  4.0 7.3 %collective-permute-start = (bf16[1,24,2304]{2,1,0:T(8,128)(2,1)}, bf16[1,24,2304]{2,1,0:T(8,128)(2,1)S(1)}, u32[]{:S(2)}, u32[]{:S(2)}) collective-permute-start(bf16[1,24,2304]{2,1,0:T(8,128)(2,1)} %param.4), channel_id=1, source_target_pairs={{0,8},{4,12},{8,0},{12,4},{16,24},{20,28},{24,16},{28,20},{1,9},{5... | collective-permute-start | bytes 331784 | tf_op jit(solution)/shard_map/ppermute | solution.py:312
  5.6 7.6 %collective-permute-start.2 = (bf16[1,24,2304]{2,1,0:T(8,128)(2,1)}, bf16[1,24,2304]{2,1,0:T(8,128)(2,1)S(1)}, u32[]{:S(2)}, u32[]{:S(2)}) collective-permute-start(bf16[1,24,2304]{2,1,0:T(8,128)(2,1)} %param.4), channel_id=1, source_target_pairs={{0,24},{4,28},{8,16},{12,20},{16,8},{20,12},{24,0},{28,4},{1,25},{... | collective-permute-start | bytes 331784 | tf_op jit(solution)/shard_map/ppermute | solution.py:312
  6.3 1.7 %copy-start = (bf16[256,24,200]{0,2,1:T(8,128)(2,1)S(1)}, bf16[256,24,200]{0,2,1:T(8,128)(2,1)}, u32[]{:S(2)}) copy-start(bf16[256,24,200]{0,2,1:T(8,128)(2,1)} %param.5) | copy-start | bytes 7372804
  8.0 5.2 %copy-start.1 = (bf16[1,24,2304]{2,1,0:T(8,128)(2,1)S(1)}, bf16[1,24,2304]{2,1,0:T(8,128)(2,1)}, u32[]{:S(2)}) copy-start(bf16[1,24,2304]{2,1,0:T(8,128)(2,1)} %param.4) | copy-start | bytes 331780
  8.0 5.5 %copy-start.2 = (s32[3]{0:T(128)S(1)}, s32[3]{0:T(128)}, u32[]{:S(2)}) copy-start(s32[3]{0:T(128)} %param.7) | copy-start | bytes 40
  13.3 1.9 %collective-permute-start.3 = (bf16[4,24,2304]{2,1,0:T(8,128)(2,1)S(1)}, bf16[4,24,2304]{2,1,0:T(8,128)(2,1)S(1)}, u32[]{:S(2)}, u32[]{:S(2)}) collective-permute-start(bf16[4,24,2304]{2,1,0:T(8,128)(2,1)S(1)} %pad_maximum_fusion.even_ref), channel_id=1, source_target_pairs={{0,4},{4,0},{8,12},{12,8},{16,20},{20,16},{24,28},{28,24},{1,5},{5... | collective-permute-start | bytes 1327112 | tf_op jit(solution)/shard_map/ppermute | solution.py:315
  23.7 11.2 %collective-permute-start.4 = (bf16[2,128,512]{2,1,0:T(8,128)(2,1)}, bf16[2,128,512]{2,1,0:T(8,128)(2,1)}, u32[]{:S(2)}, u32[]{:S(2)}) collective-permute-start(bf16[2,128,512]{2,1,0:T(8,128)(2,1)} %get-tuple-element.26), channel_id=1, source_target_pairs={{0,2},{1,3},{2,0},{3,1},{4,6},{5,7},{6,4},{7,5},{8,10},{9,11},{10,... | collective-permute-start | bytes 786440 | tf_op jit(solution)/shard_map/ppermute | solution.py:194
  25.2 9.7 %collective-permute-start.5 = (bf16[2,128,512]{2,1,0:T(8,128)(2,1)}, bf16[2,128,512]{2,1,0:T(8,128)(2,1)}, u32[]{:S(2)}, u32[]{:S(2)}) collective-permute-start(bf16[2,128,512]{2,1,0:T(8,128)(2,1)} %get-tuple-element.27), channel_id=1, source_target_pairs={{0,1},{1,0},{2,3},{3,2},{4,5},{5,4},{6,7},{7,6},{8,9},{9,8},{10,11... | collective-permute-start | bytes 786440 | tf_op jit(solution)/shard_map/ppermute | solution.py:194
  26.7 14.1 %collective-permute-start.6 = (bf16[256,512]{1,0:T(8,128)(2,1)}, bf16[256,512]{1,0:T(8,128)(2,1)}, u32[]{:S(2)}, u32[]{:S(2)}) collective-permute-start(bf16[256,512]{1,0:T(8,128)(2,1)} %get-tuple-element.28.refs_0_), channel_id=1, source_target_pairs={{0,3},{1,2},{2,1},{3,0},{4,7},{5,6},{6,5},{7,4},{8,11},{9,10},{10,... | collective-permute-start | bytes 786440 | tf_op jit(solution)/shard_map/ppermute | solution.py:194
  31.9 14.2 %collective-permute-start.7 = (bf16[256,512]{1,0:T(8,128)(2,1)}, bf16[256,512]{1,0:T(8,128)(2,1)}, u32[]{:S(2)}, u32[]{:S(2)}) collective-permute-start(bf16[256,512]{1,0:T(8,128)(2,1)} %get-tuple-element.33), channel_id=1, source_target_pairs={{0,1},{1,0},{2,3},{3,2},{4,5},{5,4},{6,7},{7,6},{8,9},{9,8},{10,11... | collective-permute-start | bytes 786440 | tf_op jit(solution)/shard_map/ppermute | solution.py:194
  33.4 12.7 %collective-permute-start.8 = (bf16[256,512]{1,0:T(8,128)(2,1)}, bf16[256,512]{1,0:T(8,128)(2,1)}, u32[]{:S(2)}, u32[]{:S(2)}) collective-permute-start(bf16[256,512]{1,0:T(8,128)(2,1)} %get-tuple-element.29.refs_2_), channel_id=1, source_target_pairs={{0,2},{1,3},{2,0},{3,1},{4,6},{5,7},{6,4},{7,5},{8,10},{9,11},{10,... | collective-permute-start | bytes 786440 | tf_op jit(solution)/shard_map/ppermute | solution.py:194
  40.3 18.6 %collective-permute-start.10 = (bf16[256,512]{1,0:T(8,128)(2,1)}, bf16[256,512]{1,0:T(8,128)(2,1)}, u32[]{:S(2)}, u32[]{:S(2)}) collective-permute-start(bf16[256,512]{1,0:T(8,128)(2,1)} %get-tuple-element.30.refs_2_), channel_id=1, source_target_pairs={{0,2},{1,3},{2,0},{3,1},{4,6},{5,7},{6,4},{7,5},{8,10},{9,11},{10,... | collective-permute-start | bytes 786440 | tf_op jit(solution)/shard_map/ppermute | solution.py:194
  46.0 9.6 %collective-permute-start.11 = (bf16[256,512]{1,0:T(8,128)(2,1)}, bf16[256,512]{1,0:T(8,128)(2,1)}, u32[]{:S(2)}, u32[]{:S(2)}) collective-permute-start(bf16[256,512]{1,0:T(8,128)(2,1)} %get-tuple-element.37), channel_id=1, source_target_pairs={{0,1},{1,0},{2,3},{3,2},{4,5},{5,4},{6,7},{7,6},{8,9},{9,8},{10,11... | collective-permute-start | bytes 786440 | tf_op jit(solution)/shard_map/ppermute | solution.py:194
  47.4 8.6 %collective-permute-start.12 = (bf16[256,512]{1,0:T(8,128)(2,1)}, bf16[256,512]{1,0:T(8,128)(2,1)}, u32[]{:S(2)}, u32[]{:S(2)}) collective-permute-start(bf16[256,512]{1,0:T(8,128)(2,1)} %get-tuple-element.38.refs_0_), channel_id=1, source_target_pairs={{0,2},{1,3},{2,0},{3,1},{4,6},{5,7},{6,4},{7,5},{8,10},{9,11},{10,... | collective-permute-start | bytes 786440 | tf_op jit(solution)/shard_map/ppermute | solution.py:194
  48.9 10.0 %collective-permute-start.9 = (bf16[256,512]{1,0:T(8,128)(2,1)}, bf16[256,512]{1,0:T(8,128)(2,1)}, u32[]{:S(2)}, u32[]{:S(2)}) collective-permute-start(bf16[256,512]{1,0:T(8,128)(2,1)} %get-tuple-element.36), channel_id=1, source_target_pairs={{0,1},{1,0},{2,3},{3,2},{4,5},{5,4},{6,7},{7,6},{8,9},{9,8},{10,11... | collective-permute-start | bytes 786440 | tf_op jit(solution)/shard_map/ppermute | solution.py:194

commit v2 on v1

--- a/solution.py
+++ b/solution.py
@@ -17,7 +17,7 @@
 
 
 def inverse_norm(mean_square):
-    return 1.0 / (jnp.sqrt(mean_square + EPS) * math.sqrt(W))
+    return lax.rsqrt(mean_square + EPS) * (1.0 / math.sqrt(W))
 
 
 def template_kernel(count_ref, tpl_ref, out_ref, scaled_ref):
@@ -228,19 +228,23 @@
             to_x, to_y, *first = lax.optimization_barrier((to_x, to_y, *arrived[0]))
             arrived[0] = tuple(first)
         arrived.append((exchange(to_x, 1, 4), exchange(to_y, 2, 4)))
-    (total,) = partial_sums(
-        tuple(range(NB)),
-        write_plain,
-        (jax.ShapeDtypeStruct((NB, slots, lags), jnp.float32),),
-        jnp.stack([me] * NB),
-        *args,
-        order=order[:1],
-    )
+    totals = []
+    order = order[:1]
+    for chunks in ((0,), (1, 2)):
+        totals += partial_sums(
+            chunks,
+            write_plain,
+            (jax.ShapeDtypeStruct((len(chunks), slots, lags), jnp.float32),),
+            jnp.stack([me] * len(chunks)),
+            *args,
+            order=order,
+        )
+        order = (totals[0], *arrived[1])
     arrived[0] += (straight,)
-    return finish(total, arrived)
-
-
-def finish_kernel(shares, total_ref, *refs):
+    return finish(totals, arrived)
+
+
+def finish_kernel(shares, first_ref, rest_ref, *refs):
     n_part = sum(shares)
     parts, out_ref, stage = refs[:n_part], refs[n_part], refs[n_part + 1]
     held = refs[n_part + 2 : 2 * n_part + 2]
@@ -251,7 +255,7 @@
     leaving = []
     at = 0
     for number, share in enumerate(shares):
-        value = total_ref[number]
+        value = rest_ref[number - 1] if number else first_ref[0]
         for index in range(at, at + share):
             arriving[index].wait()
             value = value + held[index][...].astype(jnp.float32)
@@ -267,21 +271,23 @@
         copy.wait()
 
 
-def finish(total, arrived):
+def finish(totals, arrived):
     parts = [one for group in arrived for one in group]
+    shape = (NB,) + totals[0].shape[1:]
+    whole = pl.BlockSpec(memory_space=pltpu.VMEM)
     anywhere = pl.BlockSpec(memory_space=pl.ANY)
     return pl.pallas_call(
         functools.partial(finish_kernel, [len(group) for group in arrived]),
-        out_shape=jax.ShapeDtypeStruct(total.shape, jnp.float32),
-        in_specs=[pl.BlockSpec(memory_space=pltpu.VMEM)] + [anywhere] * len(parts),
+        out_shape=jax.ShapeDtypeStruct(shape, jnp.float32),
+        in_specs=[whole, whole] + [anywhere] * len(parts),
         out_specs=anywhere,
-        scratch_shapes=[pltpu.VMEM(total.shape, jnp.float32)]
+        scratch_shapes=[pltpu.VMEM(shape, jnp.float32)]
         + [pltpu.VMEM(part.shape, part.dtype) for part in parts]
-        + [pltpu.SemaphoreType.DMA] * (len(parts) + total.shape[0]),
+        + [pltpu.SemaphoreType.DMA] * (len(parts) + NB),
         compiler_params=pltpu.CompilerParams(vmem_limit_bytes=VMEM_LIMIT),
         cost_estimate=pl.CostEstimate(flops=10**9, bytes_accessed=10**7, transcendentals=0),
         name="finish",
-    )(total, *parts)
+    )(*totals, *parts)
 
 
 def one_step(normed, segments, scales, lags, n_chan):

time: 61.7 us -> 60.8 us (0.985)
  waiting for transfers between devices: 9.7 us -> 6.67 us
  Pallas kernels: 32.8 us -> 34.8 us
    ppermute x9, waiting for transfers between devices: 3.77 us -> 0.87 us  [exchange(): return lax.ppermute(value, 'chan', [(i, i ^ step) for i in range(n_chan)])]
    pallas_call x5 -> x6, Pallas kernels: 27 us -> 29.1 us  [partial_sums(): pl.pallas_call(functools.partial(partial_kernel, chunks, len(adds), len(o...]
  transfers between devices with their start and end apart: 13 -> 13, of which waited for: 6 -> 4; matrix products, arithmetic and copies ran while one was open for 0% -> 0% of each run, Pallas kernels for 35% -> 39%
where the time goes in v2:
time: 60.8 us; the launch traced here: 60.6 us
  Pallas kernels  34.8 us (57%)
  starting transfers between devices  16.3 us (27%)
  waiting for transfers between devices  6.67 us (11%)
  local copies, waits for them, and re-layouts  1.7 us (3%)
  between operations  0.91 us (1%)
    pallas_call x6, Pallas kernels, partial_sums(): pl.pallas_call(functools.partial(partial_kernel, chunks, len(adds), len(o...  29.1 us
    ppermute x9, starting transfers between devices, exchange(): return lax.ppermute(value, 'chan', [(i, i ^ step) for i in range(n_chan)])  10.6 us
    ppermute x3, starting transfers between devices, body(): lax.ppermute(data, 'tmpl', [(i, i ^ step) for i in range(n_tmpl)])  5.62 us
    ppermute x3, waiting for transfers between devices, body(): lax.ppermute(data, 'tmpl', [(i, i ^ step) for i in range(n_tmpl)])  4.18 us
    pallas_call x1, Pallas kernels, finish(): pl.pallas_call(functools.partial(finish_kernel, [len(group) for group in...  2.4 us
    pallas_call x1, Pallas kernels, choose_blocks(): pl.pallas_call(block_kernel, out_shape=(jax.ShapeDtypeStruct((NB, held, l...  2.22 us
    unnamed x6, local copies, waits for them, and re-layouts  1.69 us
    ppermute x1, waiting for transfers between devices, body(): odd = lax.ppermute(even, 'tmpl', [(i, i ^ 1) for i in range(n_tmpl)])  1.62 us
  transfers between devices with their start and end apart: 13, of which 4 were waited for; matrix products, arithmetic and copies ran while one was open for 0% of the time, Pallas kernels for 39%

profile of v2, /device:TPU:0, one launch (start us, length us, event | category | flops | bytes accessed | tf_op | source)
XLA Modules:
  0.0 60.6 jit_solution(13650405748961299831)
XLA Ops:
  0.0 4.0 %collective-permute-start.1 = (bf16[1,24,2304]{2,1,0:T(8,128)(2,1)}, bf16[1,24,2304]{2,1,0:T(8,128)(2,1)S(1)}, u32[]{:S(2)}, u32[]{:S(2)}) collective-permute-start(bf16[1,24,2304]{2,1,0:T(8,128)(2,1)} %param.4), channel_id=1, source_target_pairs={{0,16},{4,20},{8,24},{12,28},{16,0},{20,4},{24,8},{28,12},{1,17},{... | collective-permute-start | bytes 331784 | tf_op jit(solution)/shard_map/ppermute | solution.py:318
  4.0 1.6 %collective-permute-start = (bf16[1,24,2304]{2,1,0:T(8,128)(2,1)}, bf16[1,24,2304]{2,1,0:T(8,128)(2,1)S(1)}, u32[]{:S(2)}, u32[]{:S(2)}) collective-permute-start(bf16[1,24,2304]{2,1,0:T(8,128)(2,1)} %param.4), channel_id=1, source_target_pairs={{0,8},{4,12},{8,0},{12,4},{16,24},{20,28},{24,16},{28,20},{1,9},{5... | collective-permute-start | bytes 331784 | tf_op jit(solution)/shard_map/ppermute | solution.py:318
  6.3 1.7 %copy-done = bf16[256,24,200]{0,2,1:T(8,128)(2,1)S(1)} copy-done((bf16[256,24,200]{0,2,1:T(8,128)(2,1)S(1)}, bf16[256,24,200]{0,2,1:T(8,128)(2,1)}, u32[]{:S(2)}) %copy-start) | copy-done | bytes 2457624
  8.0 1.1 %normalize_templates.1.tpl_ref = bf16[256,4800]{1,0:T(8,128)(2,1)S(1)} custom-call(s32[1]{0:T(128)S(6)} %copy.5.count_ref, bf16[24,200,256]{2,1,0:T(8,128)(2,1)S(1)} %bitcast.5), custom_call_target="tpu_custom_call" | custom-call | flops 4915200 | bytes 4915200 | tf_op jit(solution)/shard_map/normalize_templates/pallas_call | solution.py:41
  9.0 2.3 %collective-permute-done.1 = bf16[1,24,2304]{2,1,0:T(8,128)(2,1)S(1)} collective-permute-done((bf16[1,24,2304]{2,1,0:T(8,128)(2,1)}, bf16[1,24,2304]{2,1,0:T(8,128)(2,1)S(1)}, u32[]{:S(2)}, u32[]{:S(2)}) %collective-permute-start.1) | collective-permute-done | bytes 110624 | tf_op jit(solution)/shard_map/ppermute | solution.py:318
  11.3 0.0 collective-permute-done
  11.3 1.9 %collective-permute-done.2 = bf16[1,24,2304]{2,1,0:T(8,128)(2,1)S(1)} collective-permute-done((bf16[1,24,2304]{2,1,0:T(8,128)(2,1)}, bf16[1,24,2304]{2,1,0:T(8,128)(2,1)S(1)}, u32[]{:S(2)}, u32[]{:S(2)}) %collective-permute-start.2) | collective-permute-done | bytes 110624 | tf_op jit(solution)/shard_map/ppermute | solution.py:318
  13.2 0.1 pad_maximum_fusion.even_ref
  13.3 0.1 collective-permute-start.3
  13.4 0.1 pad_add_fusion.1.place_ref
  13.4 0.1 pad_add_fusion.place_ref
  13.5 1.6 %collective-permute-done.3.odd_ref = bf16[4,24,2304]{2,1,0:T(8,128)(2,1)S(1)} collective-permute-done((bf16[4,24,2304]{2,1,0:T(8,128)(2,1)S(1)}, bf16[4,24,2304]{2,1,0:T(8,128)(2,1)S(1)}, u32[]{:S(2)}, u32[]{:S(2)}) %collective-permute-start.3) | collective-permute-done | bytes 442400 | tf_op jit(solution)/shard_map/ppermute | solution.py:321
  15.1 2.2 %choose_blocks.1 = (bf16[3,24,2304]{2,1,0:T(8,128)(2,1)S(1)}, f32[3,24,2048]{2,1,0:T(8,128)S(1)}) custom-call(s32[3]{0:T(128)S(1)} %broadcast_xor_fusion.code_ref, bf16[4,24,2304]{2,1,0:T(8,128)(2,1)S(1)} %pad_maximum_fusion.even_ref, bf16[4,24,2304]{2,1,0:T(8,128)(2,1)S(1)} %collective-permute-done.3.odd_ref), custom_call_target="tpu_custom_call" | custom-call | flops 10000000000 | bytes 100000000 | tf_op jit(solution)/shard_map/choose_blocks/pallas_call | solution.py:83
  17.4 6.7 %partial_sums.6 = (bf16[2,128,512]{2,1,0:T(8,128)(2,1)}, bf16[2,128,512]{2,1,0:T(8,128)(2,1)}, bf16[256,512]{1,0:T(8,128)(2,1)}) custom-call(s32[3]{0:T(128)S(1)} %stack.27.place_ref, bf16[256,4800]{1,0:T(8,128)(2,1)S(1)} %normalize_templates.1.tpl_ref, bf16[3,24,2304]{2,1,0:T(8,128)(2,1)S(1)} %get-tuple-element.24.seg_ref, ...), custom_call_target="tpu_custom_call" | custom-call | flops 999999995904 | bytes 10000000000 | tf_op jit(solution)/shard_map/partial_sums/pallas_call | solution.py:143
  24.1 1.5 %collective-permute-start.4 = (bf16[2,128,512]{2,1,0:T(8,128)(2,1)}, bf16[2,128,512]{2,1,0:T(8,128)(2,1)}, u32[]{:S(2)}, u32[]{:S(2)}) collective-permute-start(bf16[2,128,512]{2,1,0:T(8,128)(2,1)} %get-tuple-element.26), channel_id=1, source_target_pairs={{0,2},{1,3},{2,0},{3,1},{4,6},{5,7},{6,4},{7,5},{8,10},{9,11},{10,... | collective-permute-start | bytes 786440 | tf_op jit(solution)/shard_map/ppermute | solution.py:194
  25.6 1.5 %collective-permute-start.5 = (bf16[2,128,512]{2,1,0:T(8,128)(2,1)}, bf16[2,128,512]{2,1,0:T(8,128)(2,1)}, u32[]{:S(2)}, u32[]{:S(2)}) collective-permute-start(bf16[2,128,512]{2,1,0:T(8,128)(2,1)} %get-tuple-element.27), channel_id=1, source_target_pairs={{0,1},{1,0},{2,3},{3,2},{4,5},{5,4},{6,7},{7,6},{8,9},{9,8},{10,11... | collective-permute-start | bytes 786440 | tf_op jit(solution)/shard_map/ppermute | solution.py:194
  27.1 0.4 collective-permute-start.6
  27.5 5.0 %partial_sums.7 = (bf16[256,512]{1,0:T(8,128)(2,1)}, bf16[256,512]{1,0:T(8,128)(2,1)}) custom-call(s32[2]{0:T(128)S(1)} %pad_add_fusion.place_ref, bf16[256,4800]{1,0:T(8,128)(2,1)S(1)} %normalize_templates.1.tpl_ref, bf16[3,24,2304]{2,1,0:T(8,128)(2,1)S(1)} %get-tuple-element.24.seg_ref, f32[3,24,2048]{2,1,0:T(8,128)S(1)} %get-tuple-element.25.scale_ref, ...), custom_call_target="tpu_custom_call" | custom-call | flops 999999995904 | bytes 10000000000 | tf_op jit(solution)/shard_map/partial_sums/pallas_call | solution.py:143
  32.5 1.5 %collective-permute-start.9 = (bf16[256,512]{1,0:T(8,128)(2,1)}, bf16[256,512]{1,0:T(8,128)(2,1)}, u32[]{:S(2)}, u32[]{:S(2)}) collective-permute-start(bf16[256,512]{1,0:T(8,128)(2,1)} %get-tuple-element.34), channel_id=1, source_target_pairs={{0,1},{1,0},{2,3},{3,2},{4,5},{5,4},{6,7},{7,6},{8,9},{9,8},{10,11... | collective-permute-start | bytes 786440 | tf_op jit(solution)/shard_map/ppermute | solution.py:194
  34.0 1.5 %collective-permute-start.10 = (bf16[256,512]{1,0:T(8,128)(2,1)}, bf16[256,512]{1,0:T(8,128)(2,1)}, u32[]{:S(2)}, u32[]{:S(2)}) collective-permute-start(bf16[256,512]{1,0:T(8,128)(2,1)} %get-tuple-element.29.refs_2_), channel_id=1, source_target_pairs={{0,2},{1,3},{2,0},{3,1},{4,6},{5,7},{6,4},{7,5},{8,10},{9,11},{10,... | collective-permute-start | bytes 786440 | tf_op jit(solution)/shard_map/ppermute | solution.py:194
  35.6 0.0 collective-permute-done.4.refs_0_
  35.6 0.0 collective-permute-done.5.refs_1_
  35.6 5.7 %partial_sums.8 = (bf16[256,512]{1,0:T(8,128)(2,1)}, bf16[256,512]{1,0:T(8,128)(2,1)}) custom-call(s32[2]{0:T(128)S(1)} %pad_add_fusion.place_ref, bf16[256,4800]{1,0:T(8,128)(2,1)S(1)} %normalize_templates.1.tpl_ref, bf16[3,24,2304]{2,1,0:T(8,128)(2,1)S(1)} %get-tuple-element.24.seg_ref, f32[3,24,2048]{2,1,0:T(8,128)S(1)} %get-tuple-element.25.scale_ref, ...), custom_call_target="tpu_custom_call" | custom-call | flops 999999995904 | bytes 10000000000 | tf_op jit(solution)/shard_map/partial_sums/pallas_call | solution.py:143
  41.3 1.0 %collective-permute-start.7 = (bf16[256,512]{1,0:T(8,128)(2,1)}, bf16[256,512]{1,0:T(8,128)(2,1)}, u32[]{:S(2)}, u32[]{:S(2)}) collective-permute-start(bf16[256,512]{1,0:T(8,128)(2,1)} %get-tuple-element.32), channel_id=1, source_target_pairs={{0,1},{1,0},{2,3},{3,2},{4,5},{5,4},{6,7},{7,6},{8,9},{9,8},{10,11... | collective-permute-start | bytes 786440 | tf_op jit(solution)/shard_map/ppermute | solution.py:194
  42.3 0.5 collective-permute-start.8
  42.8 5.5 %partial_sums.9 = (bf16[256,512]{1,0:T(8,128)(2,1)}, bf16[256,512]{1,0:T(8,128)(2,1)}) custom-call(s32[2]{0:T(128)S(1)} %pad_add_fusion.place_ref, bf16[256,4800]{1,0:T(8,128)(2,1)S(1)} %normalize_templates.1.tpl_ref, bf16[3,24,2304]{2,1,0:T(8,128)(2,1)S(1)} %get-tuple-element.24.seg_ref, f32[3,24,2048]{2,1,0:T(8,128)S(1)} %get-tuple-element.25.scale_ref, ...), custom_call_target="tpu_custom_call" | custom-call | flops 999999995904 | bytes 10000000000 | tf_op jit(solution)/shard_map/partial_sums/pallas_call | solution.py:143
  48.3 2.0 %partial_sums.10.refs_0_.first_ref = f32[1,256,512]{2,1,0:T(8,128)S(1)} custom-call(s32[1]{0:T(128)} %bitcast.place_ref, bf16[256,4800]{1,0:T(8,128)(2,1)S(1)} %normalize_templates.1.tpl_ref, bf16[3,24,2304]{2,1,0:T(8,128)(2,1)S(1)} %get-tuple-element.24.seg_ref, f32[3,24,2048]{2,1,0:T(8,128)S(1)} %get-tuple-element.25.scale_ref, ...), custom_call_target="tpu_custom_call" | custom-call | flops 999999995904 | bytes 10000000000 | tf_op jit(solution)/shard_map/partial_sums/pallas_call | solution.py:143
  50.3 1.1 %collective-permute-start.11 = (bf16[256,512]{1,0:T(8,128)(2,1)}, bf16[256,512]{1,0:T(8,128)(2,1)}, u32[]{:S(2)}, u32[]{:S(2)}) collective-permute-start(bf16[256,512]{1,0:T(8,128)(2,1)} %get-tuple-element.37), channel_id=1, source_target_pairs={{0,1},{1,0},{2,3},{3,2},{4,5},{5,4},{6,7},{7,6},{8,9},{9,8},{10,11... | collective-permute-start | bytes 786440 | tf_op jit(solution)/shard_map/ppermute | solution.py:194
  51.4 1.5 %collective-permute-start.12 = (bf16[256,512]{1,0:T(8,128)(2,1)}, bf16[256,512]{1,0:T(8,128)(2,1)}, u32[]{:S(2)}, u32[]{:S(2)}) collective-permute-start(bf16[256,512]{1,0:T(8,128)(2,1)} %get-tuple-element.38.refs_0_), channel_id=1, source_target_pairs={{0,2},{1,3},{2,0},{3,1},{4,6},{5,7},{6,4},{7,5},{8,10},{9,11},{10,... | collective-permute-start | bytes 786440 | tf_op jit(solution)/shard_map/ppermute | solution.py:194
  52.9 4.3 %partial_sums.11.rest_ref = f32[2,256,512]{2,1,0:T(8,128)S(1)} custom-call(s32[2]{0:T(128)S(1)} %pad_add_fusion.1.place_ref, bf16[256,4800]{1,0:T(8,128)(2,1)S(1)} %normalize_templates.1.tpl_ref, bf16[3,24,2304]{2,1,0:T(8,128)(2,1)S(1)} %get-tuple-element.24.seg_ref, f32[3,24,2048]{2,1,0:T(8,128)S(1)} %get-tuple-element.25.scale_ref, ...), custom_call_target="tpu_custom_call" | custom-call | flops 999999995904 | bytes 10000000000 | tf_op jit(solution)/shard_map/partial_sums/pallas_call | solution.py:143
  57.2 0.8 %collective-permute-done.12.refs_6_ = bf16[256,512]{1,0:T(8,128)(2,1)} collective-permute-done((bf16[256,512]{1,0:T(8,128)(2,1)}, bf16[256,512]{1,0:T(8,128)(2,1)}, u32[]{:S(2)}, u32[]{:S(2)}) %collective-permute-start.12) | collective-permute-done | bytes 262176 | tf_op jit(solution)/shard_map/ppermute | solution.py:194
  58.1 2.4 %finish.1 = f32[3,256,512]{2,1,0:T(8,128)} custom-call(f32[1,256,512]{2,1,0:T(8,128)S(1)} %partial_sums.10.refs_0_.first_ref, f32[2,256,512]{2,1,0:T(8,128)S(1)} %partial_sums.11.rest_ref, bf16[256,512]{1,0:T(8,128)(2,1)} %collective-permute-done.9.refs_0_, bf16[256,512]{1,0:T(8,128)(2,1)} %collective-permute-done.10.refs_1_, ...), custom_call_target="tpu_custom_call" | custom-call | flops 1000000000 | bytes 10000000 | tf_op jit(solution)/shard_map/finish/pallas_call | solution.py:279
  (14 shorter events, 0.0 us)
Async XLA Ops:
  0.0 11.3 %collective-permute-start.1 = (bf16[1,24,2304]{2,1,0:T(8,128)(2,1)}, bf16[1,24,2304]{2,1,0:T(8,128)(2,1)S(1)}, u32[]{:S(2)}, u32[]{:S(2)}) collective-permute-start(bf16[1,24,2304]{2,1,0:T(8,128)(2,1)} %param.4), channel_id=1, source_target_pairs={{0,16},{4,20},{8,24},{12,28},{16,0},{20,4},{24,8},{28,12},{1,17},{... | collective-permute-start | bytes 331784 | tf_op jit(solution)/shard_map/ppermute | solution.py:318
  4.0 7.3 %collective-permute-start = (bf16[1,24,2304]{2,1,0:T(8,128)(2,1)}, bf16[1,24,2304]{2,1,0:T(8,128)(2,1)S(1)}, u32[]{:S(2)}, u32[]{:S(2)}) collective-permute-start(bf16[1,24,2304]{2,1,0:T(8,128)(2,1)} %param.4), channel_id=1, source_target_pairs={{0,8},{4,12},{8,0},{12,4},{16,24},{20,28},{24,16},{28,20},{1,9},{5... | collective-permute-start | bytes 331784 | tf_op jit(solution)/shard_map/ppermute | solution.py:318
  5.6 7.6 %collective-permute-start.2 = (bf16[1,24,2304]{2,1,0:T(8,128)(2,1)}, bf16[1,24,2304]{2,1,0:T(8,128)(2,1)S(1)}, u32[]{:S(2)}, u32[]{:S(2)}) collective-permute-start(bf16[1,24,2304]{2,1,0:T(8,128)(2,1)} %param.4), channel_id=1, source_target_pairs={{0,24},{4,28},{8,16},{12,20},{16,8},{20,12},{24,0},{28,4},{1,25},{... | collective-permute-start | bytes 331784 | tf_op jit(solution)/shard_map/ppermute | solution.py:318
  6.3 1.7 %copy-start = (bf16[256,24,200]{0,2,1:T(8,128)(2,1)S(1)}, bf16[256,24,200]{0,2,1:T(8,128)(2,1)}, u32[]{:S(2)}) copy-start(bf16[256,24,200]{0,2,1:T(8,128)(2,1)} %param.5) | copy-start | bytes 7372804
  8.0 5.2 %copy-start.1 = (bf16[1,24,2304]{2,1,0:T(8,128)(2,1)S(1)}, bf16[1,24,2304]{2,1,0:T(8,128)(2,1)}, u32[]{:S(2)}) copy-start(bf16[1,24,2304]{2,1,0:T(8,128)(2,1)} %param.4) | copy-start | bytes 331780
  8.0 5.5 %copy-start.2 = (s32[3]{0:T(128)S(1)}, s32[3]{0:T(128)}, u32[]{:S(2)}) copy-start(s32[3]{0:T(128)} %param.7) | copy-start | bytes 40
  13.3 1.9 %collective-permute-start.3 = (bf16[4,24,2304]{2,1,0:T(8,128)(2,1)S(1)}, bf16[4,24,2304]{2,1,0:T(8,128)(2,1)S(1)}, u32[]{:S(2)}, u32[]{:S(2)}) collective-permute-start(bf16[4,24,2304]{2,1,0:T(8,128)(2,1)S(1)} %pad_maximum_fusion.even_ref), channel_id=1, source_target_pairs={{0,4},{4,0},{8,12},{12,8},{16,20},{20,16},{24,28},{28,24},{1,5},{5... | collective-permute-start | bytes 1327112 | tf_op jit(solution)/shard_map/ppermute | solution.py:321
  24.1 11.5 %collective-permute-start.4 = (bf16[2,128,512]{2,1,0:T(8,128)(2,1)}, bf16[2,128,512]{2,1,0:T(8,128)(2,1)}, u32[]{:S(2)}, u32[]{:S(2)}) collective-permute-start(bf16[2,128,512]{2,1,0:T(8,128)(2,1)} %get-tuple-element.26), channel_id=1, source_target_pairs={{0,2},{1,3},{2,0},{3,1},{4,6},{5,7},{6,4},{7,5},{8,10},{9,11},{10,... | collective-permute-start | bytes 786440 | tf_op jit(solution)/shard_map/ppermute | solution.py:194
  25.6 10.0 %collective-permute-start.5 = (bf16[2,128,512]{2,1,0:T(8,128)(2,1)}, bf16[2,128,512]{2,1,0:T(8,128)(2,1)}, u32[]{:S(2)}, u32[]{:S(2)}) collective-permute-start(bf16[2,128,512]{2,1,0:T(8,128)(2,1)} %get-tuple-element.27), channel_id=1, source_target_pairs={{0,1},{1,0},{2,3},{3,2},{4,5},{5,4},{6,7},{7,6},{8,9},{9,8},{10,11... | collective-permute-start | bytes 786440 | tf_op jit(solution)/shard_map/ppermute | solution.py:194
  27.1 15.7 %collective-permute-start.6 = (bf16[256,512]{1,0:T(8,128)(2,1)}, bf16[256,512]{1,0:T(8,128)(2,1)}, u32[]{:S(2)}, u32[]{:S(2)}) collective-permute-start(bf16[256,512]{1,0:T(8,128)(2,1)} %get-tuple-element.28.refs_0_), channel_id=1, source_target_pairs={{0,3},{1,2},{2,1},{3,0},{4,7},{5,6},{6,5},{7,4},{8,11},{9,10},{10,... | collective-permute-start | bytes 786440 | tf_op jit(solution)/shard_map/ppermute | solution.py:194
  32.5 17.8 %collective-permute-start.9 = (bf16[256,512]{1,0:T(8,128)(2,1)}, bf16[256,512]{1,0:T(8,128)(2,1)}, u32[]{:S(2)}, u32[]{:S(2)}) collective-permute-start(bf16[256,512]{1,0:T(8,128)(2,1)} %get-tuple-element.34), channel_id=1, source_target_pairs={{0,1},{1,0},{2,3},{3,2},{4,5},{5,4},{6,7},{7,6},{8,9},{9,8},{10,11... | collective-permute-start | bytes 786440 | tf_op jit(solution)/shard_map/ppermute | solution.py:194
  34.0 16.3 %collective-permute-start.10 = (bf16[256,512]{1,0:T(8,128)(2,1)}, bf16[256,512]{1,0:T(8,128)(2,1)}, u32[]{:S(2)}, u32[]{:S(2)}) collective-permute-start(bf16[256,512]{1,0:T(8,128)(2,1)} %get-tuple-element.29.refs_2_), channel_id=1, source_target_pairs={{0,2},{1,3},{2,0},{3,1},{4,6},{5,7},{6,4},{7,5},{8,10},{9,11},{10,... | collective-permute-start | bytes 786440 | tf_op jit(solution)/shard_map/ppermute | solution.py:194
  41.3 11.6 %collective-permute-start.7 = (bf16[256,512]{1,0:T(8,128)(2,1)}, bf16[256,512]{1,0:T(8,128)(2,1)}, u32[]{:S(2)}, u32[]{:S(2)}) collective-permute-start(bf16[256,512]{1,0:T(8,128)(2,1)} %get-tuple-element.32), channel_id=1, source_target_pairs={{0,1},{1,0},{2,3},{3,2},{4,5},{5,4},{6,7},{7,6},{8,9},{9,8},{10,11... | collective-permute-start | bytes 786440 | tf_op jit(solution)/shard_map/ppermute | solution.py:194
  42.3 10.6 %collective-permute-start.8 = (bf16[256,512]{1,0:T(8,128)(2,1)}, bf16[256,512]{1,0:T(8,128)(2,1)}, u32[]{:S(2)}, u32[]{:S(2)}) collective-permute-start(bf16[256,512]{1,0:T(8,128)(2,1)} %get-tuple-element.30.refs_2_), channel_id=1, source_target_pairs={{0,2},{1,3},{2,0},{3,1},{4,6},{5,7},{6,4},{7,5},{8,10},{9,11},{10,... | collective-permute-start | bytes 786440 | tf_op jit(solution)/shard_map/ppermute | solution.py:194
  50.3 6.9 %collective-permute-start.11 = (bf16[256,512]{1,0:T(8,128)(2,1)}, bf16[256,512]{1,0:T(8,128)(2,1)}, u32[]{:S(2)}, u32[]{:S(2)}) collective-permute-start(bf16[256,512]{1,0:T(8,128)(2,1)} %get-tuple-element.37), channel_id=1, source_target_pairs={{0,1},{1,0},{2,3},{3,2},{4,5},{5,4},{6,7},{7,6},{8,9},{9,8},{10,11... | collective-permute-start | bytes 786440 | tf_op jit(solution)/shard_map/ppermute | solution.py:194
  51.4 6.7 %collective-permute-start.12 = (bf16[256,512]{1,0:T(8,128)(2,1)}, bf16[256,512]{1,0:T(8,128)(2,1)}, u32[]{:S(2)}, u32[]{:S(2)}) collective-permute-start(bf16[256,512]{1,0:T(8,128)(2,1)} %get-tuple-element.38.refs_0_), channel_id=1, source_target_pairs={{0,2},{1,3},{2,0},{3,1},{4,6},{5,7},{6,4},{7,5},{8,10},{9,11},{10,... | collective-permute-start | bytes 786440 | tf_op jit(solution)/shard_map/ppermute | solution.py:194

commit v3 on v2

--- a/solution.py
+++ b/solution.py
@@ -252,10 +252,18 @@
     arriving = [pltpu.make_async_copy(*trio) for trio in zip(parts, held, semaphores)]
     for copy in arriving:
         copy.start()
+    bases = [
+        pltpu.make_async_copy(first_ref, stage.at[:1], semaphores[-2]),
+        pltpu.make_async_copy(rest_ref, stage.at[1:], semaphores[-1]),
+    ]
+    for copy in bases:
+        copy.start()
     leaving = []
     at = 0
     for number, share in enumerate(shares):
-        value = rest_ref[number - 1] if number else first_ref[0]
+        if number < 2:
+            bases[number].wait()
+        value = stage[number]
         for index in range(at, at + share):
             arriving[index].wait()
             value = value + held[index][...].astype(jnp.float32)
@@ -274,16 +282,15 @@
 def finish(totals, arrived):
     parts = [one for group in arrived for one in group]
     shape = (NB,) + totals[0].shape[1:]
-    whole = pl.BlockSpec(memory_space=pltpu.VMEM)
     anywhere = pl.BlockSpec(memory_space=pl.ANY)
     return pl.pallas_call(
         functools.partial(finish_kernel, [len(group) for group in arrived]),
         out_shape=jax.ShapeDtypeStruct(shape, jnp.float32),
-        in_specs=[whole, whole] + [anywhere] * len(parts),
+        in_specs=[anywhere, anywhere] + [anywhere] * len(parts),
         out_specs=anywhere,
         scratch_shapes=[pltpu.VMEM(shape, jnp.float32)]
         + [pltpu.VMEM(part.shape, part.dtype) for part in parts]
-        + [pltpu.SemaphoreType.DMA] * (len(parts) + NB),
+        + [pltpu.SemaphoreType.DMA] * (len(parts) + NB + 2),
         compiler_params=pltpu.CompilerParams(vmem_limit_bytes=VMEM_LIMIT),
         cost_estimate=pl.CostEstimate(flops=10**9, bytes_accessed=10**7, transcendentals=0),
         name="finish",

time: 60.8 us -> 60.9 us (level)
  no operation moved by 1% of the time
where the time goes in v3:
time: 60.9 us; the launch traced here: 60.6 us
  Pallas kernels  34.8 us (57%)
  starting transfers between devices  16.3 us (27%)
  waiting for transfers between devices  6.67 us (11%)
  local copies, waits for them, and re-layouts  1.7 us (3%)
  between operations  0.91 us (1%)
    pallas_call x6, Pallas kernels, partial_sums(): pl.pallas_call(functools.partial(partial_kernel, chunks, len(adds), len(o...  29.1 us
    ppermute x9, starting transfers between devices, exchange(): return lax.ppermute(value, 'chan', [(i, i ^ step) for i in range(n_chan)])  10.6 us
    ppermute x3, starting transfers between devices, body(): lax.ppermute(data, 'tmpl', [(i, i ^ step) for i in range(n_tmpl)])  5.62 us
    ppermute x3, waiting for transfers between devices, body(): lax.ppermute(data, 'tmpl', [(i, i ^ step) for i in range(n_tmpl)])  4.18 us
    pallas_call x1, Pallas kernels, finish(): pl.pallas_call(functools.partial(finish_kernel, [len(group) for group in...  2.41 us
    pallas_call x1, Pallas kernels, choose_blocks(): pl.pallas_call(block_kernel, out_shape=(jax.ShapeDtypeStruct((NB, held, l...  2.22 us
    unnamed x6, local copies, waits for them, and re-layouts  1.69 us
    ppermute x1, waiting for transfers between devices, body(): odd = lax.ppermute(even, 'tmpl', [(i, i ^ 1) for i in range(n_tmpl)])  1.62 us
  transfers between devices with their start and end apart: 13, of which 4 were waited for; matrix products, arithmetic and copies ran while one was open for 0% of the time, Pallas kernels for 39%

profile of v3, /device:TPU:0, one launch (start us, length us, event | category | flops | bytes accessed | tf_op | source)
XLA Modules:
  0.0 60.6 jit_solution(4719647188639088390)
XLA Ops:
  0.0 4.0 %collective-permute-start.1 = (bf16[1,24,2304]{2,1,0:T(8,128)(2,1)}, bf16[1,24,2304]{2,1,0:T(8,128)(2,1)S(1)}, u32[]{:S(2)}, u32[]{:S(2)}) collective-permute-start(bf16[1,24,2304]{2,1,0:T(8,128)(2,1)} %param.4), channel_id=1, source_target_pairs={{0,16},{4,20},{8,24},{12,28},{16,0},{20,4},{24,8},{28,12},{1,17},{... | collective-permute-start | bytes 331784 | tf_op jit(solution)/shard_map/ppermute | solution.py:325
  4.0 1.6 %collective-permute-start = (bf16[1,24,2304]{2,1,0:T(8,128)(2,1)}, bf16[1,24,2304]{2,1,0:T(8,128)(2,1)S(1)}, u32[]{:S(2)}, u32[]{:S(2)}) collective-permute-start(bf16[1,24,2304]{2,1,0:T(8,128)(2,1)} %param.4), channel_id=1, source_target_pairs={{0,8},{4,12},{8,0},{12,4},{16,24},{20,28},{24,16},{28,20},{1,9},{5... | collective-permute-start | bytes 331784 | tf_op jit(solution)/shard_map/ppermute | solution.py:325
  5.6 0.0 collective-permute-start.2
  6.3 1.7 %copy-done = bf16[256,24,200]{0,2,1:T(8,128)(2,1)S(1)} copy-done((bf16[256,24,200]{0,2,1:T(8,128)(2,1)S(1)}, bf16[256,24,200]{0,2,1:T(8,128)(2,1)}, u32[]{:S(2)}) %copy-start) | copy-done | bytes 2457624
  8.0 1.1 %normalize_templates.1.tpl_ref = bf16[256,4800]{1,0:T(8,128)(2,1)S(1)} custom-call(s32[1]{0:T(128)S(6)} %copy.5.count_ref, bf16[24,200,256]{2,1,0:T(8,128)(2,1)S(1)} %bitcast.5), custom_call_target="tpu_custom_call" | custom-call | flops 4915200 | bytes 4915200 | tf_op jit(solution)/shard_map/normalize_templates/pallas_call | solution.py:41
  9.0 2.3 %collective-permute-done.1 = bf16[1,24,2304]{2,1,0:T(8,128)(2,1)S(1)} collective-permute-done((bf16[1,24,2304]{2,1,0:T(8,128)(2,1)}, bf16[1,24,2304]{2,1,0:T(8,128)(2,1)S(1)}, u32[]{:S(2)}, u32[]{:S(2)}) %collective-permute-start.1) | collective-permute-done | bytes 110624 | tf_op jit(solution)/shard_map/ppermute | solution.py:325
  11.3 0.0 collective-permute-done
  11.3 1.9 %collective-permute-done.2 = bf16[1,24,2304]{2,1,0:T(8,128)(2,1)S(1)} collective-permute-done((bf16[1,24,2304]{2,1,0:T(8,128)(2,1)}, bf16[1,24,2304]{2,1,0:T(8,128)(2,1)S(1)}, u32[]{:S(2)}, u32[]{:S(2)}) %collective-permute-start.2) | collective-permute-done | bytes 110624 | tf_op jit(solution)/shard_map/ppermute | solution.py:325
  13.2 0.1 pad_maximum_fusion.even_ref
  13.3 0.1 collective-permute-start.3
  13.4 0.1 pad_add_fusion.1.place_ref
  13.4 0.1 pad_add_fusion.place_ref
  13.5 1.6 %collective-permute-done.3.odd_ref = bf16[4,24,2304]{2,1,0:T(8,128)(2,1)S(1)} collective-permute-done((bf16[4,24,2304]{2,1,0:T(8,128)(2,1)S(1)}, bf16[4,24,2304]{2,1,0:T(8,128)(2,1)S(1)}, u32[]{:S(2)}, u32[]{:S(2)}) %collective-permute-start.3) | collective-permute-done | bytes 442400 | tf_op jit(solution)/shard_map/ppermute | solution.py:328
  15.1 2.2 %choose_blocks.1 = (bf16[3,24,2304]{2,1,0:T(8,128)(2,1)S(1)}, f32[3,24,2048]{2,1,0:T(8,128)S(1)}) custom-call(s32[3]{0:T(128)S(1)} %broadcast_xor_fusion.code_ref, bf16[4,24,2304]{2,1,0:T(8,128)(2,1)S(1)} %pad_maximum_fusion.even_ref, bf16[4,24,2304]{2,1,0:T(8,128)(2,1)S(1)} %collective-permute-done.3.odd_ref), custom_call_target="tpu_custom_call" | custom-call | flops 10000000000 | bytes 100000000 | tf_op jit(solution)/shard_map/choose_blocks/pallas_call | solution.py:83
  17.4 6.7 %partial_sums.6 = (bf16[2,128,512]{2,1,0:T(8,128)(2,1)}, bf16[2,128,512]{2,1,0:T(8,128)(2,1)}, bf16[256,512]{1,0:T(8,128)(2,1)}) custom-call(s32[3]{0:T(128)S(1)} %stack.27.place_ref, bf16[256,4800]{1,0:T(8,128)(2,1)S(1)} %normalize_templates.1.tpl_ref, bf16[3,24,2304]{2,1,0:T(8,128)(2,1)S(1)} %get-tuple-element.24.seg_ref, ...), custom_call_target="tpu_custom_call" | custom-call | flops 999999995904 | bytes 10000000000 | tf_op jit(solution)/shard_map/partial_sums/pallas_call | solution.py:143
  24.1 1.5 %collective-permute-start.4 = (bf16[2,128,512]{2,1,0:T(8,128)(2,1)}, bf16[2,128,512]{2,1,0:T(8,128)(2,1)}, u32[]{:S(2)}, u32[]{:S(2)}) collective-permute-start(bf16[2,128,512]{2,1,0:T(8,128)(2,1)} %get-tuple-element.26), channel_id=1, source_target_pairs={{0,2},{1,3},{2,0},{3,1},{4,6},{5,7},{6,4},{7,5},{8,10},{9,11},{10,... | collective-permute-start | bytes 786440 | tf_op jit(solution)/shard_map/ppermute | solution.py:194
  25.6 1.5 %collective-permute-start.5 = (bf16[2,128,512]{2,1,0:T(8,128)(2,1)}, bf16[2,128,512]{2,1,0:T(8,128)(2,1)}, u32[]{:S(2)}, u32[]{:S(2)}) collective-permute-start(bf16[2,128,512]{2,1,0:T(8,128)(2,1)} %get-tuple-element.27), channel_id=1, source_target_pairs={{0,1},{1,0},{2,3},{3,2},{4,5},{5,4},{6,7},{7,6},{8,9},{9,8},{10,11... | collective-permute-start | bytes 786440 | tf_op jit(solution)/shard_map/ppermute | solution.py:194
  27.1 0.4 collective-permute-start.6
  27.5 5.0 %partial_sums.7 = (bf16[256,512]{1,0:T(8,128)(2,1)}, bf16[256,512]{1,0:T(8,128)(2,1)}) custom-call(s32[2]{0:T(128)S(1)} %pad_add_fusion.place_ref, bf16[256,4800]{1,0:T(8,128)(2,1)S(1)} %normalize_templates.1.tpl_ref, bf16[3,24,2304]{2,1,0:T(8,128)(2,1)S(1)} %get-tuple-element.24.seg_ref, f32[3,24,2048]{2,1,0:T(8,128)S(1)} %get-tuple-element.25.scale_ref, ...), custom_call_target="tpu_custom_call" | custom-call | flops 999999995904 | bytes 10000000000 | tf_op jit(solution)/shard_map/partial_sums/pallas_call | solution.py:143
  32.5 1.5 %collective-permute-start.9 = (bf16[256,512]{1,0:T(8,128)(2,1)}, bf16[256,512]{1,0:T(8,128)(2,1)}, u32[]{:S(2)}, u32[]{:S(2)}) collective-permute-start(bf16[256,512]{1,0:T(8,128)(2,1)} %get-tuple-element.34), channel_id=1, source_target_pairs={{0,1},{1,0},{2,3},{3,2},{4,5},{5,4},{6,7},{7,6},{8,9},{9,8},{10,11... | collective-permute-start | bytes 786440 | tf_op jit(solution)/shard_map/ppermute | solution.py:194
  34.0 1.5 %collective-permute-start.10 = (bf16[256,512]{1,0:T(8,128)(2,1)}, bf16[256,512]{1,0:T(8,128)(2,1)}, u32[]{:S(2)}, u32[]{:S(2)}) collective-permute-start(bf16[256,512]{1,0:T(8,128)(2,1)} %get-tuple-element.29.refs_2_), channel_id=1, source_target_pairs={{0,2},{1,3},{2,0},{3,1},{4,6},{5,7},{6,4},{7,5},{8,10},{9,11},{10,... | collective-permute-start | bytes 786440 | tf_op jit(solution)/shard_map/ppermute | solution.py:194
  35.6 0.0 collective-permute-done.5.refs_1_
  35.6 5.7 %partial_sums.8 = (bf16[256,512]{1,0:T(8,128)(2,1)}, bf16[256,512]{1,0:T(8,128)(2,1)}) custom-call(s32[2]{0:T(128)S(1)} %pad_add_fusion.place_ref, bf16[256,4800]{1,0:T(8,128)(2,1)S(1)} %normalize_templates.1.tpl_ref, bf16[3,24,2304]{2,1,0:T(8,128)(2,1)S(1)} %get-tuple-element.24.seg_ref, f32[3,24,2048]{2,1,0:T(8,128)S(1)} %get-tuple-element.25.scale_ref, ...), custom_call_target="tpu_custom_call" | custom-call | flops 999999995904 | bytes 10000000000 | tf_op jit(solution)/shard_map/partial_sums/pallas_call | solution.py:143
  41.3 1.0 %collective-permute-start.7 = (bf16[256,512]{1,0:T(8,128)(2,1)}, bf16[256,512]{1,0:T(8,128)(2,1)}, u32[]{:S(2)}, u32[]{:S(2)}) collective-permute-start(bf16[256,512]{1,0:T(8,128)(2,1)} %get-tuple-element.32), channel_id=1, source_target_pairs={{0,1},{1,0},{2,3},{3,2},{4,5},{5,4},{6,7},{7,6},{8,9},{9,8},{10,11... | collective-permute-start | bytes 786440 | tf_op jit(solution)/shard_map/ppermute | solution.py:194
  42.3 0.5 collective-permute-start.8
  42.8 5.5 %partial_sums.9 = (bf16[256,512]{1,0:T(8,128)(2,1)}, bf16[256,512]{1,0:T(8,128)(2,1)}) custom-call(s32[2]{0:T(128)S(1)} %pad_add_fusion.place_ref, bf16[256,4800]{1,0:T(8,128)(2,1)S(1)} %normalize_templates.1.tpl_ref, bf16[3,24,2304]{2,1,0:T(8,128)(2,1)S(1)} %get-tuple-element.24.seg_ref, f32[3,24,2048]{2,1,0:T(8,128)S(1)} %get-tuple-element.25.scale_ref, ...), custom_call_target="tpu_custom_call" | custom-call | flops 999999995904 | bytes 10000000000 | tf_op jit(solution)/shard_map/partial_sums/pallas_call | solution.py:143
  48.3 2.0 %partial_sums.10.refs_0_.first_ref = f32[1,256,512]{2,1,0:T(8,128)S(1)} custom-call(s32[1]{0:T(128)} %bitcast.place_ref, bf16[256,4800]{1,0:T(8,128)(2,1)S(1)} %normalize_templates.1.tpl_ref, bf16[3,24,2304]{2,1,0:T(8,128)(2,1)S(1)} %get-tuple-element.24.seg_ref, f32[3,24,2048]{2,1,0:T(8,128)S(1)} %get-tuple-element.25.scale_ref, ...), custom_call_target="tpu_custom_call" | custom-call | flops 999999995904 | bytes 10000000000 | tf_op jit(solution)/shard_map/partial_sums/pallas_call | solution.py:143
  50.3 1.1 %collective-permute-start.11 = (bf16[256,512]{1,0:T(8,128)(2,1)}, bf16[256,512]{1,0:T(8,128)(2,1)}, u32[]{:S(2)}, u32[]{:S(2)}) collective-permute-start(bf16[256,512]{1,0:T(8,128)(2,1)} %get-tuple-element.37), channel_id=1, source_target_pairs={{0,1},{1,0},{2,3},{3,2},{4,5},{5,4},{6,7},{7,6},{8,9},{9,8},{10,11... | collective-permute-start | bytes 786440 | tf_op jit(solution)/shard_map/ppermute | solution.py:194
  51.4 1.5 %collective-permute-start.12 = (bf16[256,512]{1,0:T(8,128)(2,1)}, bf16[256,512]{1,0:T(8,128)(2,1)}, u32[]{:S(2)}, u32[]{:S(2)}) collective-permute-start(bf16[256,512]{1,0:T(8,128)(2,1)} %get-tuple-element.38.refs_0_), channel_id=1, source_target_pairs={{0,2},{1,3},{2,0},{3,1},{4,6},{5,7},{6,4},{7,5},{8,10},{9,11},{10,... | collective-permute-start | bytes 786440 | tf_op jit(solution)/shard_map/ppermute | solution.py:194
  52.9 4.3 %partial_sums.11.rest_ref = f32[2,256,512]{2,1,0:T(8,128)S(1)} custom-call(s32[2]{0:T(128)S(1)} %pad_add_fusion.1.place_ref, bf16[256,4800]{1,0:T(8,128)(2,1)S(1)} %normalize_templates.1.tpl_ref, bf16[3,24,2304]{2,1,0:T(8,128)(2,1)S(1)} %get-tuple-element.24.seg_ref, f32[3,24,2048]{2,1,0:T(8,128)S(1)} %get-tuple-element.25.scale_ref, ...), custom_call_target="tpu_custom_call" | custom-call | flops 999999995904 | bytes 10000000000 | tf_op jit(solution)/shard_map/partial_sums/pallas_call | solution.py:143
  57.2 0.8 %collective-permute-done.12.refs_6_ = bf16[256,512]{1,0:T(8,128)(2,1)} collective-permute-done((bf16[256,512]{1,0:T(8,128)(2,1)}, bf16[256,512]{1,0:T(8,128)(2,1)}, u32[]{:S(2)}, u32[]{:S(2)}) %collective-permute-start.12) | collective-permute-done | bytes 262176 | tf_op jit(solution)/shard_map/ppermute | solution.py:194
  58.1 2.4 %finish.1 = f32[3,256,512]{2,1,0:T(8,128)} custom-call(f32[1,256,512]{2,1,0:T(8,128)S(1)} %partial_sums.10.refs_0_.first_ref, f32[2,256,512]{2,1,0:T(8,128)S(1)} %partial_sums.11.rest_ref, bf16[256,512]{1,0:T(8,128)(2,1)} %collective-permute-done.9.refs_0_, bf16[256,512]{1,0:T(8,128)(2,1)} %collective-permute-done.10.refs_1_, ...), custom_call_target="tpu_custom_call" | custom-call | flops 1000000000 | bytes 10000000 | tf_op jit(solution)/shard_map/finish/pallas_call | solution.py:286
  (14 shorter events, 0.0 us)
Async XLA Ops:
  0.0 11.3 %collective-permute-start.1 = (bf16[1,24,2304]{2,1,0:T(8,128)(2,1)}, bf16[1,24,2304]{2,1,0:T(8,128)(2,1)S(1)}, u32[]{:S(2)}, u32[]{:S(2)}) collective-permute-start(bf16[1,24,2304]{2,1,0:T(8,128)(2,1)} %param.4), channel_id=1, source_target_pairs={{0,16},{4,20},{8,24},{12,28},{16,0},{20,4},{24,8},{28,12},{1,17},{... | collective-permute-start | bytes 331784 | tf_op jit(solution)/shard_map/ppermute | solution.py:325
  4.0 7.3 %collective-permute-start = (bf16[1,24,2304]{2,1,0:T(8,128)(2,1)}, bf16[1,24,2304]{2,1,0:T(8,128)(2,1)S(1)}, u32[]{:S(2)}, u32[]{:S(2)}) collective-permute-start(bf16[1,24,2304]{2,1,0:T(8,128)(2,1)} %param.4), channel_id=1, source_target_pairs={{0,8},{4,12},{8,0},{12,4},{16,24},{20,28},{24,16},{28,20},{1,9},{5... | collective-permute-start | bytes 331784 | tf_op jit(solution)/shard_map/ppermute | solution.py:325
  5.6 7.6 %collective-permute-start.2 = (bf16[1,24,2304]{2,1,0:T(8,128)(2,1)}, bf16[1,24,2304]{2,1,0:T(8,128)(2,1)S(1)}, u32[]{:S(2)}, u32[]{:S(2)}) collective-permute-start(bf16[1,24,2304]{2,1,0:T(8,128)(2,1)} %param.4), channel_id=1, source_target_pairs={{0,24},{4,28},{8,16},{12,20},{16,8},{20,12},{24,0},{28,4},{1,25},{... | collective-permute-start | bytes 331784 | tf_op jit(solution)/shard_map/ppermute | solution.py:325
  6.3 1.7 %copy-start = (bf16[256,24,200]{0,2,1:T(8,128)(2,1)S(1)}, bf16[256,24,200]{0,2,1:T(8,128)(2,1)}, u32[]{:S(2)}) copy-start(bf16[256,24,200]{0,2,1:T(8,128)(2,1)} %param.5) | copy-start | bytes 7372804
  8.0 5.2 %copy-start.1 = (bf16[1,24,2304]{2,1,0:T(8,128)(2,1)S(1)}, bf16[1,24,2304]{2,1,0:T(8,128)(2,1)}, u32[]{:S(2)}) copy-start(bf16[1,24,2304]{2,1,0:T(8,128)(2,1)} %param.4) | copy-start | bytes 331780
  8.0 5.5 %copy-start.2 = (s32[3]{0:T(128)S(1)}, s32[3]{0:T(128)}, u32[]{:S(2)}) copy-start(s32[3]{0:T(128)} %param.7) | copy-start | bytes 40
  13.3 1.9 %collective-permute-start.3 = (bf16[4,24,2304]{2,1,0:T(8,128)(2,1)S(1)}, bf16[4,24,2304]{2,1,0:T(8,128)(2,1)S(1)}, u32[]{:S(2)}, u32[]{:S(2)}) collective-permute-start(bf16[4,24,2304]{2,1,0:T(8,128)(2,1)S(1)} %pad_maximum_fusion.even_ref), channel_id=1, source_target_pairs={{0,4},{4,0},{8,12},{12,8},{16,20},{20,16},{24,28},{28,24},{1,5},{5... | collective-permute-start | bytes 1327112 | tf_op jit(solution)/shard_map/ppermute | solution.py:328
  24.1 11.5 %collective-permute-start.4 = (bf16[2,128,512]{2,1,0:T(8,128)(2,1)}, bf16[2,128,512]{2,1,0:T(8,128)(2,1)}, u32[]{:S(2)}, u32[]{:S(2)}) collective-permute-start(bf16[2,128,512]{2,1,0:T(8,128)(2,1)} %get-tuple-element.26), channel_id=1, source_target_pairs={{0,2},{1,3},{2,0},{3,1},{4,6},{5,7},{6,4},{7,5},{8,10},{9,11},{10,... | collective-permute-start | bytes 786440 | tf_op jit(solution)/shard_map/ppermute | solution.py:194
  25.6 10.0 %collective-permute-start.5 = (bf16[2,128,512]{2,1,0:T(8,128)(2,1)}, bf16[2,128,512]{2,1,0:T(8,128)(2,1)}, u32[]{:S(2)}, u32[]{:S(2)}) collective-permute-start(bf16[2,128,512]{2,1,0:T(8,128)(2,1)} %get-tuple-element.27), channel_id=1, source_target_pairs={{0,1},{1,0},{2,3},{3,2},{4,5},{5,4},{6,7},{7,6},{8,9},{9,8},{10,11... | collective-permute-start | bytes 786440 | tf_op jit(solution)/shard_map/ppermute | solution.py:194
  27.1 15.7 %collective-permute-start.6 = (bf16[256,512]{1,0:T(8,128)(2,1)}, bf16[256,512]{1,0:T(8,128)(2,1)}, u32[]{:S(2)}, u32[]{:S(2)}) collective-permute-start(bf16[256,512]{1,0:T(8,128)(2,1)} %get-tuple-element.28.refs_0_), channel_id=1, source_target_pairs={{0,3},{1,2},{2,1},{3,0},{4,7},{5,6},{6,5},{7,4},{8,11},{9,10},{10,... | collective-permute-start | bytes 786440 | tf_op jit(solution)/shard_map/ppermute | solution.py:194
  32.5 17.8 %collective-permute-start.9 = (bf16[256,512]{1,0:T(8,128)(2,1)}, bf16[256,512]{1,0:T(8,128)(2,1)}, u32[]{:S(2)}, u32[]{:S(2)}) collective-permute-start(bf16[256,512]{1,0:T(8,128)(2,1)} %get-tuple-element.34), channel_id=1, source_target_pairs={{0,1},{1,0},{2,3},{3,2},{4,5},{5,4},{6,7},{7,6},{8,9},{9,8},{10,11... | collective-permute-start | bytes 786440 | tf_op jit(solution)/shard_map/ppermute | solution.py:194
  34.0 16.3 %collective-permute-start.10 = (bf16[256,512]{1,0:T(8,128)(2,1)}, bf16[256,512]{1,0:T(8,128)(2,1)}, u32[]{:S(2)}, u32[]{:S(2)}) collective-permute-start(bf16[256,512]{1,0:T(8,128)(2,1)} %get-tuple-element.29.refs_2_), channel_id=1, source_target_pairs={{0,2},{1,3},{2,0},{3,1},{4,6},{5,7},{6,4},{7,5},{8,10},{9,11},{10,... | collective-permute-start | bytes 786440 | tf_op jit(solution)/shard_map/ppermute | solution.py:194
  41.3 11.6 %collective-permute-start.7 = (bf16[256,512]{1,0:T(8,128)(2,1)}, bf16[256,512]{1,0:T(8,128)(2,1)}, u32[]{:S(2)}, u32[]{:S(2)}) collective-permute-start(bf16[256,512]{1,0:T(8,128)(2,1)} %get-tuple-element.32), channel_id=1, source_target_pairs={{0,1},{1,0},{2,3},{3,2},{4,5},{5,4},{6,7},{7,6},{8,9},{9,8},{10,11... | collective-permute-start | bytes 786440 | tf_op jit(solution)/shard_map/ppermute | solution.py:194
  42.3 10.6 %collective-permute-start.8 = (bf16[256,512]{1,0:T(8,128)(2,1)}, bf16[256,512]{1,0:T(8,128)(2,1)}, u32[]{:S(2)}, u32[]{:S(2)}) collective-permute-start(bf16[256,512]{1,0:T(8,128)(2,1)} %get-tuple-element.30.refs_2_), channel_id=1, source_target_pairs={{0,2},{1,3},{2,0},{3,1},{4,6},{5,7},{6,4},{7,5},{8,10},{9,11},{10,... | collective-permute-start | bytes 786440 | tf_op jit(solution)/shard_map/ppermute | solution.py:194
  50.3 6.9 %collective-permute-start.11 = (bf16[256,512]{1,0:T(8,128)(2,1)}, bf16[256,512]{1,0:T(8,128)(2,1)}, u32[]{:S(2)}, u32[]{:S(2)}) collective-permute-start(bf16[256,512]{1,0:T(8,128)(2,1)} %get-tuple-element.37), channel_id=1, source_target_pairs={{0,1},{1,0},{2,3},{3,2},{4,5},{5,4},{6,7},{7,6},{8,9},{9,8},{10,11... | collective-permute-start | bytes 786440 | tf_op jit(solution)/shard_map/ppermute | solution.py:194
  51.4 6.7 %collective-permute-start.12 = (bf16[256,512]{1,0:T(8,128)(2,1)}, bf16[256,512]{1,0:T(8,128)(2,1)}, u32[]{:S(2)}, u32[]{:S(2)}) collective-permute-start(bf16[256,512]{1,0:T(8,128)(2,1)} %get-tuple-element.38.refs_0_), channel_id=1, source_target_pairs={{0,2},{1,3},{2,0},{3,1},{4,6},{5,7},{6,4},{7,5},{8,10},{9,11},{10,... | collective-permute-start | bytes 786440 | tf_op jit(solution)/shard_map/ppermute | solution.py:194
